TPU v7x, 32 devices: a whole 2x2x4 slice. The times are simulated.
32 devices in a mesh: groups: 2 (over y), tm: 4 (over x, core), gz: 4 (over z).
Axes of the slice: x: 2, y: 2, z: 4, core: 2. Of those that a mesh axis runs over, the one named last changes fastest.
Arguments:
- initial_state: float32 [32, 16, 256], P(('groups', 'gz')), parts along dimension 0, may hold values from -6 to 6
- start_guess: float32 [4, 32, 16, 256], P('tm', ('groups', 'gz')), parts along dimension 1, may hold values from -6 to 6
- control: float32 [4, 32, 16, 256], P('tm', ('groups', 'gz')), parts along dimension 1, may hold values from -6 to 6
- reaction_rate: float32 [4, 32, 16, 256], P('tm', ('groups', 'gz')), parts along dimension 1, may hold values from 0.05 to 8
Outputs:
- node_states: float32 [4, 3, 32, 16, 256], P('tm', None, ('groups', 'gz')), parts along dimension 2
There are 2 independent parts, one for each index of `groups`. A program takes and returns all parts, laid end to end along the dimension named above; each array names one. Nothing has to cross between parts.
All inputs are finite; a program needn't handle non-finite values.
Results may differ from a plain program's by a relative error of at most 0.0001.
Values sent between devices are 32-bit elements; how exact they have to be, the bound alone decides.
A program may use at most 64 MiB of HBM per device.

v0:
```python
import math

import jax
import jax.numpy as jnp
from jax import lax
from jax.sharding import PartitionSpec as P

ITERS = 2


root_six = math.sqrt(6.0)
radau_matrix = (
    (
        (88.0 - 7.0 * root_six) / 360.0,
        (296.0 - 169.0 * root_six) / 1800.0,
        (-2.0 + 3.0 * root_six) / 225.0,
    ),
    (
        (296.0 + 169.0 * root_six) / 1800.0,
        (88.0 + 7.0 * root_six) / 360.0,
        (-2.0 - 3.0 * root_six) / 225.0,
    ),
    ((16.0 - root_six) / 36.0, (16.0 + root_six) / 36.0, 1.0 / 9.0),
)
diffusion = 0.1


def with_halo(cells, sides, width):
    for axis, dim in sides:
        count = lax.axis_size(axis)
        ends = count - 1
        head = lax.slice_in_dim(cells, 0, width, axis=dim)
        tail = lax.slice_in_dim(cells, cells.shape[dim] - width, cells.shape[dim], axis=dim)
        cells = jnp.concatenate(
            [
                lax.ppermute(tail, axis, [(i, (i + 1) % count) for i in range(ends)]),
                cells,
                lax.ppermute(head, axis, [((i + 1) % count, i) for i in range(ends)]),
            ],
            axis=dim,
        )
    return cells


def from_behind(array, axis, by):
    peers = lax.axis_size(axis)
    pairs = [(i, i + by) for i in range(peers) if 0 <= i + by < peers]
    return lax.ppermute(array, axis, pairs)


def laplace_padded(padded):
    middle = padded[..., 1:-1, :, :]
    planar = jnp.pad(middle, ((0, 0),) * (middle.ndim - 2) + ((1, 1), (1, 1)))
    summed = padded[..., 2:, :, :] + padded[..., :-2, :, :]
    summed = summed + planar[..., 2:, 1:-1] + planar[..., :-2, 1:-1]
    summed = summed + planar[..., 1:-1, 2:] + planar[..., 1:-1, :-2]
    return summed - 6.0 * middle


def forcing(states, laplace, control, rate):
    return diffusion * laplace + jnp.tanh(states) + control - rate * states


def integrate(values):
    return jnp.stack(
        [
            radau_matrix[row_index][0] * values[0]
            + radau_matrix[row_index][1] * values[1]
            + radau_matrix[row_index][2] * values[2]
            for row_index in range(3)
        ]
    )


def restrict(values):
    width = values.shape[-1]
    rows_added = values[..., 0::2, :] + values[..., 1::2, :]
    pair_sum = (
        lax.broadcasted_iota(jnp.int32, (width, width // 2), 0) // 2
        == lax.broadcasted_iota(jnp.int32, (width, width // 2), 1)
    ).astype(jnp.float32)
    summed = jnp.matmul(rows_added, pair_sum, precision=lax.Precision.HIGHEST)
    return 0.25 * summed


def prolong(values):
    return jnp.repeat(jnp.repeat(values, 2, axis=-2), 2, axis=-1)


def laplace_halo(values):
    padded = with_halo(values, (("gz", 1),), 1)
    return laplace_padded(padded)


def per_device(initial_state, start_guess, control, reaction_rate):
    slices = lax.axis_size("tm")
    leading = lax.axis_index("tm") == 0
    diagonal = jnp.asarray([radau_matrix[index][index] for index in range(3)], jnp.float32).reshape(
        3, 1, 1, 1
    )
    control_here = control[0]
    rate_here = reaction_rate[0]
    node_values = jnp.broadcast_to(start_guess[0], (3,) + start_guess.shape[1:])
    slice_start = jnp.where(leading, initial_state, start_guess[0])
    coarse_first = restrict(initial_state)
    coarse_rate = restrict(rate_here)
    coarse_scale = 1.0 / (1.0 + diagonal * coarse_rate)
    for number in range(ITERS):
        laplace_now = laplace_halo(node_values)
        integral = integrate(forcing(node_values, laplace_now, control_here, rate_here))
        swept_nodes = (slice_start + integral + diagonal * rate_here * node_values) / (
            1.0 + diagonal * rate_here
        )
        swept_laplace = laplace_halo(swept_nodes)
        fine_sum = integrate(forcing(swept_nodes, swept_laplace, control_here, rate_here))
        coarse = restrict(swept_nodes)
        offset = coarse_scale * (restrict(fine_sum) + diagonal * coarse_rate * coarse)

        def relay_step(counter, current):
            ending = coarse_scale[2] * current + offset[2]
            return jnp.where(leading, coarse_first, from_behind(ending, "tm", 1))

        coarse_start = lax.fori_loop(
            0,
            slices - 1,
            relay_step,
            jnp.where(leading, coarse_first, jnp.zeros_like(coarse_first)),
        )
        correction = coarse_scale * coarse_start + offset - coarse
        node_values = swept_nodes + prolong(correction)
        if number + 1 < ITERS:
            received = from_behind(node_values[2], "tm", 1)
            slice_start = jnp.where(leading, initial_state, received)
    return node_values[None]


def solution(mesh):
    in_specs = (
        P(("groups", "gz"), None, None),
        P("tm", ("groups", "gz"), None, None),
        P("tm", ("groups", "gz"), None, None),
        P("tm", ("groups", "gz"), None, None),
    )
    out_specs = P("tm", None, ("groups", "gz"), None, None)
    return jax.shard_map(
        per_device, mesh=mesh, in_specs=in_specs, out_specs=out_specs, check_vma=False
    )
```

profile of v0, /device:TPU:30, one launch (start us, length us, event | category | flops | bytes accessed | tf_op | source)
XLA Modules:
  0.0 78.4 jit_solution(14464720563812499819)
XLA Ops:
  2.1 4.5 %collective-permute-start.2 = (f32[3,1,16,256]{3,2,1,0:T(8,128)S(1)}, f32[3,1,16,256]{3,2,1,0:T(8,128)S(1)}, u32[]{:S(2)}, u32[]{:S(2)}) collective-permute-start(f32[3,1,16,256]{3,2,1,0:T(8,128)S(1)} %broadcast_in_dim.36), channel_id=1, source_target_pairs={{1,0},{2,1},{3,2},{5,4},{6,5},{7,6},{9,8},{10,9},{11,10},{13,12},{... | collective-permute-start | bytes 147464 | tf_op jit(solution)/shard_map/ppermute | solution.py:38
  14.0 2.4 %collective-permute-start.4 = (f32[3,1,16,256]{3,2,1,0:T(8,128)S(1)}, f32[3,1,16,256]{3,2,1,0:T(8,128)S(1)}, u32[]{:S(2)}, u32[]{:S(2)}) collective-permute-start(f32[3,1,16,256]{3,2,1,0:T(8,128)S(1)} %get-tuple-element.108), channel_id=1, source_target_pairs={{1,0},{2,1},{3,2},{5,4},{6,5},{7,6},{9,8},{10,9},{11,10},{13,12},{... | collective-permute-start | bytes 147464 | tf_op jit(solution)/shard_map/ppermute | solution.py:38
  16.3 1.3 %collective-permute-start.5 = (f32[3,1,16,256]{3,2,1,0:T(8,128)S(1)}, f32[3,1,16,256]{3,2,1,0:T(8,128)S(1)}, u32[]{:S(2)}, u32[]{:S(2)}) collective-permute-start(f32[3,1,16,256]{3,2,1,0:T(8,128)S(1)} %get-tuple-element.109), channel_id=1, source_target_pairs={{0,1},{1,2},{2,3},{4,5},{5,6},{6,7},{8,9},{9,10},{10,11},{12,13},{... | collective-permute-start | bytes 147464 | tf_op jit(solution)/shard_map/ppermute | solution.py:36
  18.1 4.3 %collective-permute-done.5 = f32[3,1,16,256]{3,2,1,0:T(8,128)S(1)} collective-permute-done((f32[3,1,16,256]{3,2,1,0:T(8,128)S(1)}, f32[3,1,16,256]{3,2,1,0:T(8,128)S(1)}, u32[]{:S(2)}, u32[]{:S(2)}) %collective-permute-start.5) | collective-permute-done | bytes 49184 | tf_op jit(solution)/shard_map/ppermute | solution.py:36
  23.2 15.2 %while.20 = (s32[]{:T(128)}, f32[4,8,128]{2,1,0:T(8,128)S(1)}, pred[]{:T(512)}, f32[3,4,8,128]{3,2,1,0:T(8,128)S(1)}, f32[3,4,8,128]{3,2,1,0:T(8,128)S(1)}, /*index=5*/f32[4,8,128]{2,1,0:T(8,128)S(1)}, s32[]{:T(128)}) while((s32[]{:T(128)}, f32[4,8,128]{2,1,0:T(8,128)S(1)}, pred[]{:T(512)}, f32[3,4,8,128]{3,2,1,0:T(8,128)S(1)}, ...), condition=%wide.region_1.2_spmd, body=%wide.region_0.1_spmd.sunk | while | flops 12290 | bytes 180342 | solution.py:123
  23.2 1.9 %collective-permute-start = (f32[4,8,128]{2,1,0:T(8,128)S(1)}, f32[4,8,128]{2,1,0:T(8,128)S(1)}, u32[]{:S(2)}, u32[]{:S(2)}) collective-permute-start(f32[4,8,128]{2,1,0:T(8,128)S(1)} %bitcast_add_fusion.4), channel_id=1, source_target_pairs={{0,4},{4,8},{8,12},{1,5},{5,9},{9,13},{2,6},{6,10},{10,14},{3,7},{... | collective-permute-start | bytes 49160 | tf_op jit(solution)/shard_map/while/body/eval_jaxpr/ppermute | solution.py:48
  25.1 3.1 %collective-permute-done = f32[4,8,128]{2,1,0:T(8,128)S(1)} collective-permute-done((f32[4,8,128]{2,1,0:T(8,128)S(1)}, f32[4,8,128]{2,1,0:T(8,128)S(1)}, u32[]{:S(2)}, u32[]{:S(2)}) %collective-permute-start) | collective-permute-done | bytes 16416 | tf_op jit(solution)/shard_map/while/body/eval_jaxpr/ppermute | solution.py:48
  28.3 1.9 %collective-permute-start = (f32[4,8,128]{2,1,0:T(8,128)S(1)}, f32[4,8,128]{2,1,0:T(8,128)S(1)}, u32[]{:S(2)}, u32[]{:S(2)}) collective-permute-start(f32[4,8,128]{2,1,0:T(8,128)S(1)} %bitcast_add_fusion.4), channel_id=1, source_target_pairs={{0,4},{4,8},{8,12},{1,5},{5,9},{9,13},{2,6},{6,10},{10,14},{3,7},{... | collective-permute-start | bytes 49160 | tf_op jit(solution)/shard_map/while/body/eval_jaxpr/ppermute | solution.py:48
  30.2 3.1 %collective-permute-done = f32[4,8,128]{2,1,0:T(8,128)S(1)} collective-permute-done((f32[4,8,128]{2,1,0:T(8,128)S(1)}, f32[4,8,128]{2,1,0:T(8,128)S(1)}, u32[]{:S(2)}, u32[]{:S(2)}) %collective-permute-start) | collective-permute-done | bytes 16416 | tf_op jit(solution)/shard_map/while/body/eval_jaxpr/ppermute | solution.py:48
  33.3 1.9 %collective-permute-start = (f32[4,8,128]{2,1,0:T(8,128)S(1)}, f32[4,8,128]{2,1,0:T(8,128)S(1)}, u32[]{:S(2)}, u32[]{:S(2)}) collective-permute-start(f32[4,8,128]{2,1,0:T(8,128)S(1)} %bitcast_add_fusion.4), channel_id=1, source_target_pairs={{0,4},{4,8},{8,12},{1,5},{5,9},{9,13},{2,6},{6,10},{10,14},{3,7},{... | collective-permute-start | bytes 49160 | tf_op jit(solution)/shard_map/while/body/eval_jaxpr/ppermute | solution.py:48
  35.3 3.1 %collective-permute-done = f32[4,8,128]{2,1,0:T(8,128)S(1)} collective-permute-done((f32[4,8,128]{2,1,0:T(8,128)S(1)}, f32[4,8,128]{2,1,0:T(8,128)S(1)}, u32[]{:S(2)}, u32[]{:S(2)}) %collective-permute-start) | collective-permute-done | bytes 16416 | tf_op jit(solution)/shard_map/while/body/eval_jaxpr/ppermute | solution.py:48
  39.9 2.4 %collective-permute-start.7 = (f32[3,1,16,256]{3,2,1,0:T(8,128)S(1)}, f32[3,1,16,256]{3,2,1,0:T(8,128)S(1)}, u32[]{:S(2)}, u32[]{:S(2)}) collective-permute-start(f32[3,1,16,256]{3,2,1,0:T(8,128)S(1)} %get-tuple-element.103), channel_id=1, source_target_pairs={{1,0},{2,1},{3,2},{5,4},{6,5},{7,6},{9,8},{10,9},{11,10},{13,12},{... | collective-permute-start | bytes 147464 | tf_op jit(solution)/shard_map/ppermute | solution.py:38
  42.3 1.3 %collective-permute-start.8 = (f32[3,1,16,256]{3,2,1,0:T(8,128)S(1)}, f32[3,1,16,256]{3,2,1,0:T(8,128)S(1)}, u32[]{:S(2)}, u32[]{:S(2)}) collective-permute-start(f32[3,1,16,256]{3,2,1,0:T(8,128)S(1)} %get-tuple-element.104), channel_id=1, source_target_pairs={{0,1},{1,2},{2,3},{4,5},{5,6},{6,7},{8,9},{9,10},{10,11},{12,13},{... | collective-permute-start | bytes 147464 | tf_op jit(solution)/shard_map/ppermute | solution.py:36
  43.6 1.9 %collective-permute-start.6 = (f32[4,16,256]{2,1,0:T(8,128)S(1)}, f32[4,16,256]{2,1,0:T(8,128)S(1)}, u32[]{:S(2)}, u32[]{:S(2)}) collective-permute-start(f32[4,16,256]{2,1,0:T(8,128)S(1)} %slice_bitcast_fusion), channel_id=1, source_target_pairs={{0,4},{4,8},{8,12},{1,5},{5,9},{9,13},{2,6},{6,10},{10,14},{3,7},{... | collective-permute-start | bytes 196616 | tf_op jit(solution)/shard_map/ppermute | solution.py:48
  46.0 2.3 %collective-permute-done.8 = f32[3,1,16,256]{3,2,1,0:T(8,128)S(1)} collective-permute-done((f32[3,1,16,256]{3,2,1,0:T(8,128)S(1)}, f32[3,1,16,256]{3,2,1,0:T(8,128)S(1)}, u32[]{:S(2)}, u32[]{:S(2)}) %collective-permute-start.8) | collective-permute-done | bytes 49184 | tf_op jit(solution)/shard_map/ppermute | solution.py:36
  49.6 4.5 %collective-permute-start.9 = (f32[3,1,16,256]{3,2,1,0:T(8,128)S(1)}, f32[3,1,16,256]{3,2,1,0:T(8,128)S(1)}, u32[]{:S(2)}, u32[]{:S(2)}) collective-permute-start(f32[3,1,16,256]{3,2,1,0:T(8,128)S(1)} %get-tuple-element.98), channel_id=1, source_target_pairs={{1,0},{2,1},{3,2},{5,4},{6,5},{7,6},{9,8},{10,9},{11,10},{13,12},{... | collective-permute-start | bytes 147464 | tf_op jit(solution)/shard_map/ppermute | solution.py:38
  55.9 4.3 %collective-permute-done.10 = f32[3,1,16,256]{3,2,1,0:T(8,128)S(1)} collective-permute-done((f32[3,1,16,256]{3,2,1,0:T(8,128)S(1)}, f32[3,1,16,256]{3,2,1,0:T(8,128)S(1)}, u32[]{:S(2)}, u32[]{:S(2)}) %collective-permute-start.10) | collective-permute-done | bytes 49184 | tf_op jit(solution)/shard_map/ppermute | solution.py:36
  61.0 15.2 %while.21 = (s32[]{:T(128)}, f32[4,8,128]{2,1,0:T(8,128)S(1)}, pred[]{:T(512)}, f32[3,4,8,128]{3,2,1,0:T(8,128)S(1)}, f32[3,4,8,128]{3,2,1,0:T(8,128)S(1)}, /*index=5*/f32[4,8,128]{2,1,0:T(8,128)S(1)}, s32[]{:T(128)}) while((s32[]{:T(128)}, f32[4,8,128]{2,1,0:T(8,128)S(1)}, pred[]{:T(512)}, f32[3,4,8,128]{3,2,1,0:T(8,128)S(1)}, ...), condition=%wide.region_3.4_spmd, body=%wide.region_2.3_spmd.sunk | while | flops 12290 | bytes 180342 | solution.py:123
  61.0 1.9 %collective-permute-start.1 = (f32[4,8,128]{2,1,0:T(8,128)S(1)}, f32[4,8,128]{2,1,0:T(8,128)S(1)}, u32[]{:S(2)}, u32[]{:S(2)}) collective-permute-start(f32[4,8,128]{2,1,0:T(8,128)S(1)} %bitcast_add_fusion.5), channel_id=1, source_target_pairs={{0,4},{4,8},{8,12},{1,5},{5,9},{9,13},{2,6},{6,10},{10,14},{3,7},{... | collective-permute-start | bytes 49160 | tf_op jit(solution)/shard_map/while/body/eval_jaxpr/ppermute | solution.py:48
  62.9 3.1 %collective-permute-done.1 = f32[4,8,128]{2,1,0:T(8,128)S(1)} collective-permute-done((f32[4,8,128]{2,1,0:T(8,128)S(1)}, f32[4,8,128]{2,1,0:T(8,128)S(1)}, u32[]{:S(2)}, u32[]{:S(2)}) %collective-permute-start.1) | collective-permute-done | bytes 16416 | tf_op jit(solution)/shard_map/while/body/eval_jaxpr/ppermute | solution.py:48
  66.1 1.9 %collective-permute-start.1 = (f32[4,8,128]{2,1,0:T(8,128)S(1)}, f32[4,8,128]{2,1,0:T(8,128)S(1)}, u32[]{:S(2)}, u32[]{:S(2)}) collective-permute-start(f32[4,8,128]{2,1,0:T(8,128)S(1)} %bitcast_add_fusion.5), channel_id=1, source_target_pairs={{0,4},{4,8},{8,12},{1,5},{5,9},{9,13},{2,6},{6,10},{10,14},{3,7},{... | collective-permute-start | bytes 49160 | tf_op jit(solution)/shard_map/while/body/eval_jaxpr/ppermute | solution.py:48
  68.0 3.1 %collective-permute-done.1 = f32[4,8,128]{2,1,0:T(8,128)S(1)} collective-permute-done((f32[4,8,128]{2,1,0:T(8,128)S(1)}, f32[4,8,128]{2,1,0:T(8,128)S(1)}, u32[]{:S(2)}, u32[]{:S(2)}) %collective-permute-start.1) | collective-permute-done | bytes 16416 | tf_op jit(solution)/shard_map/while/body/eval_jaxpr/ppermute | solution.py:48
  71.2 1.9 %collective-permute-start.1 = (f32[4,8,128]{2,1,0:T(8,128)S(1)}, f32[4,8,128]{2,1,0:T(8,128)S(1)}, u32[]{:S(2)}, u32[]{:S(2)}) collective-permute-start(f32[4,8,128]{2,1,0:T(8,128)S(1)} %bitcast_add_fusion.5), channel_id=1, source_target_pairs={{0,4},{4,8},{8,12},{1,5},{5,9},{9,13},{2,6},{6,10},{10,14},{3,7},{... | collective-permute-start | bytes 49160 | tf_op jit(solution)/shard_map/while/body/eval_jaxpr/ppermute | solution.py:48
  73.1 3.1 %collective-permute-done.1 = f32[4,8,128]{2,1,0:T(8,128)S(1)} collective-permute-done((f32[4,8,128]{2,1,0:T(8,128)S(1)}, f32[4,8,128]{2,1,0:T(8,128)S(1)}, u32[]{:S(2)}, u32[]{:S(2)}) %collective-permute-start.1) | collective-permute-done | bytes 16416 | tf_op jit(solution)/shard_map/while/body/eval_jaxpr/ppermute | solution.py:48
  (87 shorter events, 18.5 us)
Async XLA Ops:
  0.0 13.6 %copy-start.4 = (f32[3]{0:T(128)S(1)}, f32[3]{0:T(128)}, u32[]{:S(2)}) copy-start(f32[3]{0:T(128)} %constant.75.clone) | copy-start | bytes 40
  0.0 13.6 %copy-start.1 = (f32[1,4,16,256]{3,2,1,0:T(8,128)S(1)}, f32[1,4,16,256]{3,2,1,0:T(8,128)}, u32[]{:S(2)}) copy-start(f32[1,4,16,256]{3,2,1,0:T(8,128)} %param.10) | copy-start | bytes 196612
  0.0 13.6 %copy-start = (f32[1,4,16,256]{3,2,1,0:T(8,128)S(1)}, f32[1,4,16,256]{3,2,1,0:T(8,128)}, u32[]{:S(2)}) copy-start(f32[1,4,16,256]{3,2,1,0:T(8,128)} %param.12) | copy-start | bytes 196612
  0.0 13.3 %copy-start.2 = (f32[1,4,16,256]{3,2,1,0:T(8,128)S(1)}, f32[1,4,16,256]{3,2,1,0:T(8,128)}, u32[]{:S(2)}) copy-start(f32[1,4,16,256]{3,2,1,0:T(8,128)} %param.11) | copy-start | bytes 196612
  0.8 11.6 %collective-permute-start.3 = (f32[3,1,16,256]{3,2,1,0:T(8,128)S(1)}, f32[3,1,16,256]{3,2,1,0:T(8,128)S(1)}, u32[]{:S(2)}, u32[]{:S(2)}) collective-permute-start(f32[3,1,16,256]{3,2,1,0:T(8,128)S(1)} %broadcast_in_dim.37), channel_id=1, source_target_pairs={{0,1},{1,2},{2,3},{4,5},{5,6},{6,7},{8,9},{9,10},{10,11},{12,13},{... | collective-permute-start | bytes 147464 | tf_op jit(solution)/shard_map/ppermute | solution.py:36
  2.1 10.3 %collective-permute-start.2 = (f32[3,1,16,256]{3,2,1,0:T(8,128)S(1)}, f32[3,1,16,256]{3,2,1,0:T(8,128)S(1)}, u32[]{:S(2)}, u32[]{:S(2)}) collective-permute-start(f32[3,1,16,256]{3,2,1,0:T(8,128)S(1)} %broadcast_in_dim.36), channel_id=1, source_target_pairs={{1,0},{2,1},{3,2},{5,4},{6,5},{7,6},{9,8},{10,9},{11,10},{13,12},{... | collective-permute-start | bytes 147464 | tf_op jit(solution)/shard_map/ppermute | solution.py:38
  14.0 4.1 %collective-permute-start.4 = (f32[3,1,16,256]{3,2,1,0:T(8,128)S(1)}, f32[3,1,16,256]{3,2,1,0:T(8,128)S(1)}, u32[]{:S(2)}, u32[]{:S(2)}) collective-permute-start(f32[3,1,16,256]{3,2,1,0:T(8,128)S(1)} %get-tuple-element.108), channel_id=1, source_target_pairs={{1,0},{2,1},{3,2},{5,4},{6,5},{7,6},{9,8},{10,9},{11,10},{13,12},{... | collective-permute-start | bytes 147464 | tf_op jit(solution)/shard_map/ppermute | solution.py:38
  16.3 6.0 %collective-permute-start.5 = (f32[3,1,16,256]{3,2,1,0:T(8,128)S(1)}, f32[3,1,16,256]{3,2,1,0:T(8,128)S(1)}, u32[]{:S(2)}, u32[]{:S(2)}) collective-permute-start(f32[3,1,16,256]{3,2,1,0:T(8,128)S(1)} %get-tuple-element.109), channel_id=1, source_target_pairs={{0,1},{1,2},{2,3},{4,5},{5,6},{6,7},{8,9},{9,10},{10,11},{12,13},{... | collective-permute-start | bytes 147464 | tf_op jit(solution)/shard_map/ppermute | solution.py:36
  23.2 5.1 %collective-permute-start = (f32[4,8,128]{2,1,0:T(8,128)S(1)}, f32[4,8,128]{2,1,0:T(8,128)S(1)}, u32[]{:S(2)}, u32[]{:S(2)}) collective-permute-start(f32[4,8,128]{2,1,0:T(8,128)S(1)} %bitcast_add_fusion.4), channel_id=1, source_target_pairs={{0,4},{4,8},{8,12},{1,5},{5,9},{9,13},{2,6},{6,10},{10,14},{3,7},{... | collective-permute-start | bytes 49160 | tf_op jit(solution)/shard_map/while/body/eval_jaxpr/ppermute | solution.py:48
  28.3 5.1 %collective-permute-start = (f32[4,8,128]{2,1,0:T(8,128)S(1)}, f32[4,8,128]{2,1,0:T(8,128)S(1)}, u32[]{:S(2)}, u32[]{:S(2)}) collective-permute-start(f32[4,8,128]{2,1,0:T(8,128)S(1)} %bitcast_add_fusion.4), channel_id=1, source_target_pairs={{0,4},{4,8},{8,12},{1,5},{5,9},{9,13},{2,6},{6,10},{10,14},{3,7},{... | collective-permute-start | bytes 49160 | tf_op jit(solution)/shard_map/while/body/eval_jaxpr/ppermute | solution.py:48
  33.3 5.1 %collective-permute-start = (f32[4,8,128]{2,1,0:T(8,128)S(1)}, f32[4,8,128]{2,1,0:T(8,128)S(1)}, u32[]{:S(2)}, u32[]{:S(2)}) collective-permute-start(f32[4,8,128]{2,1,0:T(8,128)S(1)} %bitcast_add_fusion.4), channel_id=1, source_target_pairs={{0,4},{4,8},{8,12},{1,5},{5,9},{9,13},{2,6},{6,10},{10,14},{3,7},{... | collective-permute-start | bytes 49160 | tf_op jit(solution)/shard_map/while/body/eval_jaxpr/ppermute | solution.py:48
  39.9 9.3 %copy-start.3 = (f32[4,16,256]{2,1,0:T(8,128)S(1)}, f32[4,16,256]{2,1,0:T(8,128)}, u32[]{:S(2)}) copy-start(f32[4,16,256]{2,1,0:T(8,128)} %param.9) | copy-start | bytes 196612
  39.9 6.0 %collective-permute-start.7 = (f32[3,1,16,256]{3,2,1,0:T(8,128)S(1)}, f32[3,1,16,256]{3,2,1,0:T(8,128)S(1)}, u32[]{:S(2)}, u32[]{:S(2)}) collective-permute-start(f32[3,1,16,256]{3,2,1,0:T(8,128)S(1)} %get-tuple-element.103), channel_id=1, source_target_pairs={{1,0},{2,1},{3,2},{5,4},{6,5},{7,6},{9,8},{10,9},{11,10},{13,12},{... | collective-permute-start | bytes 147464 | tf_op jit(solution)/shard_map/ppermute | solution.py:38
  42.3 6.0 %collective-permute-start.8 = (f32[3,1,16,256]{3,2,1,0:T(8,128)S(1)}, f32[3,1,16,256]{3,2,1,0:T(8,128)S(1)}, u32[]{:S(2)}, u32[]{:S(2)}) collective-permute-start(f32[3,1,16,256]{3,2,1,0:T(8,128)S(1)} %get-tuple-element.104), channel_id=1, source_target_pairs={{0,1},{1,2},{2,3},{4,5},{5,6},{6,7},{8,9},{9,10},{10,11},{12,13},{... | collective-permute-start | bytes 147464 | tf_op jit(solution)/shard_map/ppermute | solution.py:36
  43.6 5.6 %collective-permute-start.6 = (f32[4,16,256]{2,1,0:T(8,128)S(1)}, f32[4,16,256]{2,1,0:T(8,128)S(1)}, u32[]{:S(2)}, u32[]{:S(2)}) collective-permute-start(f32[4,16,256]{2,1,0:T(8,128)S(1)} %slice_bitcast_fusion), channel_id=1, source_target_pairs={{0,4},{4,8},{8,12},{1,5},{5,9},{9,13},{2,6},{6,10},{10,14},{3,7},{... | collective-permute-start | bytes 196616 | tf_op jit(solution)/shard_map/ppermute | solution.py:48
  49.6 6.3 %collective-permute-start.9 = (f32[3,1,16,256]{3,2,1,0:T(8,128)S(1)}, f32[3,1,16,256]{3,2,1,0:T(8,128)S(1)}, u32[]{:S(2)}, u32[]{:S(2)}) collective-permute-start(f32[3,1,16,256]{3,2,1,0:T(8,128)S(1)} %get-tuple-element.98), channel_id=1, source_target_pairs={{1,0},{2,1},{3,2},{5,4},{6,5},{7,6},{9,8},{10,9},{11,10},{13,12},{... | collective-permute-start | bytes 147464 | tf_op jit(solution)/shard_map/ppermute | solution.py:38
  54.2 6.0 %collective-permute-start.10 = (f32[3,1,16,256]{3,2,1,0:T(8,128)S(1)}, f32[3,1,16,256]{3,2,1,0:T(8,128)S(1)}, u32[]{:S(2)}, u32[]{:S(2)}) collective-permute-start(f32[3,1,16,256]{3,2,1,0:T(8,128)S(1)} %get-tuple-element.99), channel_id=1, source_target_pairs={{0,1},{1,2},{2,3},{4,5},{5,6},{6,7},{8,9},{9,10},{10,11},{12,13},{... | collective-permute-start | bytes 147464 | tf_op jit(solution)/shard_map/ppermute | solution.py:36
  61.0 5.1 %collective-permute-start.1 = (f32[4,8,128]{2,1,0:T(8,128)S(1)}, f32[4,8,128]{2,1,0:T(8,128)S(1)}, u32[]{:S(2)}, u32[]{:S(2)}) collective-permute-start(f32[4,8,128]{2,1,0:T(8,128)S(1)} %bitcast_add_fusion.5), channel_id=1, source_target_pairs={{0,4},{4,8},{8,12},{1,5},{5,9},{9,13},{2,6},{6,10},{10,14},{3,7},{... | collective-permute-start | bytes 49160 | tf_op jit(solution)/shard_map/while/body/eval_jaxpr/ppermute | solution.py:48
  66.1 5.1 %collective-permute-start.1 = (f32[4,8,128]{2,1,0:T(8,128)S(1)}, f32[4,8,128]{2,1,0:T(8,128)S(1)}, u32[]{:S(2)}, u32[]{:S(2)}) collective-permute-start(f32[4,8,128]{2,1,0:T(8,128)S(1)} %bitcast_add_fusion.5), channel_id=1, source_target_pairs={{0,4},{4,8},{8,12},{1,5},{5,9},{9,13},{2,6},{6,10},{10,14},{3,7},{... | collective-permute-start | bytes 49160 | tf_op jit(solution)/shard_map/while/body/eval_jaxpr/ppermute | solution.py:48
  71.2 5.1 %collective-permute-start.1 = (f32[4,8,128]{2,1,0:T(8,128)S(1)}, f32[4,8,128]{2,1,0:T(8,128)S(1)}, u32[]{:S(2)}, u32[]{:S(2)}) collective-permute-start(f32[4,8,128]{2,1,0:T(8,128)S(1)} %bitcast_add_fusion.5), channel_id=1, source_target_pairs={{0,4},{4,8},{8,12},{1,5},{5,9},{9,13},{2,6},{6,10},{10,14},{3,7},{... | collective-permute-start | bytes 49160 | tf_op jit(solution)/shard_map/while/body/eval_jaxpr/ppermute | solution.py:48
where the time goes:
time: 79.3 us; the launch traced here: 78.4 us
  starting transfers between devices  32.4 us (41%)
  waiting for transfers between devices  30.5 us (38%)
  local copies, waits for them, and re-layouts  9 us (11%)
  other arithmetic  4.02 us (5%)
  matrix products  1.99 us (3%)
    ppermute x7, waiting for transfers between devices, from_behind(): return lax.ppermute(array, axis, pairs)  19.5 us
    ppermute x4, starting transfers between devices, with_halo(): lax.ppermute(head, axis, [((i + 1) % count, i) for i in range(ends)])  13.8 us
    ppermute x7, starting transfers between devices, from_behind(): return lax.ppermute(array, axis, pairs)  13.4 us
    ppermute x4, waiting for transfers between devices, with_halo(): lax.ppermute(tail, axis, [(i, (i + 1) % count) for i in range(ends)])  10.8 us
    ppermute x4, starting transfers between devices, with_halo(): lax.ppermute(tail, axis, [(i, (i + 1) % count) for i in range(ends)])  5.16 us
    slice x12, local copies, waits for them, and re-layouts, restrict(): rows_added = values[..., 0::2, :] + values[..., 1::2, :]  4.31 us
    dot_general x6, matrix products, restrict(): summed = jnp.matmul(rows_added, pair_sum, precision=lax.Precision.HIGHEST)  1.99 us
    reshape x5, local copies, waits for them, and re-layouts, prolong(): return jnp.repeat(jnp.repeat(values, 2, axis=-2), 2, axis=-1)  1.82 us
  transfers between devices with their start and end apart: 15, of which 12 were waited for; matrix products, arithmetic and copies ran while one was open for 9% of the time, Pallas kernels for 0%

commit v1 on v0

v1 whole, which is shorter than its diff:
```python
import functools
import math

import jax
import jax.numpy as jnp
from jax import lax
from jax.experimental import pallas as pl
from jax.experimental.pallas import tpu as pltpu
from jax.sharding import PartitionSpec as P

ITERS = 2

root_six = math.sqrt(6.0)
Q = (
    (
        (88.0 - 7.0 * root_six) / 360.0,
        (296.0 - 169.0 * root_six) / 1800.0,
        (-2.0 + 3.0 * root_six) / 225.0,
    ),
    (
        (296.0 + 169.0 * root_six) / 1800.0,
        (88.0 + 7.0 * root_six) / 360.0,
        (-2.0 - 3.0 * root_six) / 225.0,
    ),
    ((16.0 - root_six) / 36.0, (16.0 + root_six) / 36.0, 1.0 / 9.0),
)
D = tuple(Q[m][m] for m in range(3))
ROW = tuple(sum(Q[m]) for m in range(3))
diffusion = 0.1


def kernel(
    slices,
    slabs,
    init_ref,
    guess_ref,
    control_ref,
    rate_ref,
    out_ref,
    raw,
    halo_raw,
    swept_buf,
    swept_halo,
    coarse_buf,
    coarse_halo,
    corr_buf,
    corr_halo,
    end_in,
    scale_buf,
    scale_in,
    offset_buf,
    offset_in,
    out_buf,
    in_sem,
    out_sem,
    guess_send,
    guess_recv,
    swept_send,
    swept_recv,
    coarse_send,
    coarse_recv,
    corr_send,
    corr_recv,
    end_send,
    end_recv,
    scale_send,
    scale_recv,
    offset_send,
    offset_recv,
):
    t = lax.axis_index("tm")
    z = lax.axis_index("gz")
    layers, width, depth_rows = raw.shape[2], raw.shape[4], raw.shape[3]
    rows = depth_rows // 2
    has_above = z < slabs - 1
    has_below = z > 0

    sources = (guess_ref.at[0], rate_ref.at[0], control_ref.at[0], init_ref)
    loads = [
        [
            pltpu.make_async_copy(
                source.at[:, :, pl.ds(half * width, width)], raw.at[field, half], in_sem.at[field, half]
            )
            for half in range(2)
        ]
        for field, source in enumerate(sources)
    ]
    for pair in loads:
        for load in pair:
            load.start()

    @pl.when(z == 0)
    def _():
        halo_raw[0] = jnp.zeros_like(halo_raw[0])
        swept_halo[0] = jnp.zeros_like(swept_halo[0])
        corr_halo[0] = jnp.zeros_like(corr_halo[0])
        for it in range(ITERS):
            coarse_halo[it, 0] = jnp.zeros_like(coarse_halo[it, 0])

    @pl.when(z == slabs - 1)
    def _():
        halo_raw[1] = jnp.zeros_like(halo_raw[1])
        swept_halo[1] = jnp.zeros_like(swept_halo[1])
        corr_halo[1] = jnp.zeros_like(corr_halo[1])
        for it in range(ITERS):
            coarse_halo[it, 1] = jnp.zeros_like(coarse_halo[it, 1])

    barrier = pltpu.get_barrier_semaphore()

    def greet(condition, device):
        @pl.when(condition)
        def _():
            pl.semaphore_signal(barrier, inc=1, device_id=device, device_id_type=pl.DeviceIdType.MESH)

    greet(has_above, {"gz": z + 1})
    greet(has_below, {"gz": z - 1})
    for d in range(1, slices):
        greet(t >= d, {"tm": t - d})
    pl.semaphore_wait(
        barrier,
        has_above.astype(jnp.int32) + has_below.astype(jnp.int32) + (slices - 1 - t),
    )

    pending = []

    def remote(src, dst, send, recv, device, sends, receives):
        copy = pltpu.make_async_remote_copy(
            src_ref=src,
            dst_ref=dst,
            send_sem=send,
            recv_sem=recv,
            device_id=device,
            device_id_type=pl.DeviceIdType.MESH,
        )

        @pl.when(sends)
        def _():
            copy.start()

        def sent():
            @pl.when(sends)
            def _():
                copy.wait_send()

        def arrived():
            @pl.when(receives)
            def _():
                copy.wait_recv()

        pending.append(sent)
        return arrived

    def to_above(src, dst, send, recv):
        return remote(src, dst, send, recv, {"gz": z + 1}, has_above, has_below)

    def to_below(src, dst, send, recv):
        return remote(src, dst, send, recv, {"gz": z - 1}, has_below, has_above)

    def to_later(d, src, dst, send, recv):
        return remote(src, dst, send, recv, {"tm": t + d}, t + d < slices, t >= d)

    guess_arrived = []
    for half in range(2):
        columns = pl.ds(half * width, width)
        guess_arrived.append(
            to_above(
                guess_ref.at[0, layers - 1, :, columns],
                halo_raw.at[0, half],
                guess_send.at[0, half],
                guess_recv.at[0, half],
            )
        )
        guess_arrived.append(
            to_below(
                guess_ref.at[0, 0, :, columns],
                halo_raw.at[1, half],
                guess_send.at[1, half],
                guess_recv.at[1, half],
            )
        )

    lane = lax.broadcasted_iota(jnp.int32, (layers * rows, width), 1)

    def take(array, index):
        flat = array.reshape(-1, width)
        picked = jnp.take_along_axis(
            flat, index[: flat.shape[0]], axis=1, mode="promise_in_bounds"
        )
        return picked.reshape(array.shape)

    even_index = (2 * lane) % width
    odd_index = even_index + 1
    low_index = lane // 2
    high_index = low_index + width // 2
    lane3 = lax.broadcasted_iota(jnp.int32, (layers, rows, width), 2)
    row3 = lax.broadcasted_iota(jnp.int32, (layers, rows, width), 1)

    def split(low, high):
        front = lane3[: low.shape[0]] < width // 2
        return [
            jnp.where(front, take(low, index), take(high, index))
            for index in (even_index, odd_index)
        ]

    def parities(ref):
        out = []
        for px in range(2):
            low = ref[0, :, pl.ds(px, rows, stride=2), :]
            high = ref[1, :, pl.ds(px, rows, stride=2), :]
            out += split(low, high)
        return out

    def halo_parities(side):
        out = []
        for px in range(2):
            low = halo_raw[side, 0, pl.ds(px, rows, stride=2), :]
            high = halo_raw[side, 1, pl.ds(px, rows, stride=2), :]
            out += split(low[None], high[None])
        return out

    def down(v):
        return jnp.where(row3 == 0, 0.0, pltpu.roll(v, 1, 1))

    def up(v):
        return jnp.where(row3 == rows - 1, 0.0, pltpu.roll(v, rows - 1, 1))

    def right(v):
        return jnp.where(lane3 == 0, 0.0, pltpu.roll(v, 1, 2))

    def left(v):
        return jnp.where(lane3 == width - 1, 0.0, pltpu.roll(v, width - 1, 2))

    def planar(v):
        a, b, c, d = v
        return [
            (c + down(c)) + (b + right(b)),
            (d + down(d)) + (a + left(a)),
            (a + up(a)) + (d + right(d)),
            (b + up(b)) + (c + left(c)),
        ]

    def inner(v):
        below = jnp.concatenate([jnp.zeros_like(v[:1]), v[:-1]], 0)
        above = jnp.concatenate([v[1:], jnp.zeros_like(v[:1])], 0)
        return below + above

    def outer(low, high):
        gap = jnp.zeros((layers - 2, rows, width), jnp.float32)
        return jnp.concatenate([low, gap, high], 0)

    def total(v):
        return (v[0] + v[1]) + (v[2] + v[3])

    for load in loads[0]:
        load.wait()
    guess = parities(raw.at[0])
    for load in loads[1]:
        load.wait()
    rate = parities(raw.at[1])
    coarse_rate = 0.25 * total(rate)
    scale = [1.0 / (1.0 + D[m] * coarse_rate) for m in range(3)]
    scale_buf[...] = scale[2]
    scale_arrived = {
        d: to_later(d, scale_buf, scale_in.at[d - 1], scale_send.at[d - 1], scale_recv.at[d - 1])
        for d in range(1, slices)
    }
    for load in loads[2]:
        load.wait()
    control = parities(raw.at[2])
    for load in loads[3]:
        load.wait()
    initial = parities(raw.at[3])
    coarse_first = 0.25 * total(initial)
    coarse_control = 0.25 * total(control)
    leading = t == 0
    start = [jnp.where(leading, initial[p], guess[p]) for p in range(4)]
    inverse = [[1.0 / (1.0 + D[m] * rate[p]) for p in range(4)] for m in range(3)]

    def force_inside(v):
        flat = planar(v)
        return [
            diffusion * (flat[p] + inner(v[p]) - 6.0 * v[p])
            + jnp.tanh(v[p])
            + control[p]
            - rate[p] * v[p]
            for p in range(4)
        ]

    force = force_inside(guess)
    for arrived in guess_arrived:
        arrived()
    low, high = halo_parities(0), halo_parities(1)
    force = [force[p] + diffusion * outer(low[p], high[p]) for p in range(4)]
    swept = [
        [
            (start[p] + ROW[m] * force[p] + D[m] * rate[p] * guess[p]) * inverse[m][p]
            for p in range(4)
        ]
        for m in range(3)
    ]

    for it in range(ITERS):
        coarse = [0.25 * total(swept[m]) for m in range(3)]
        for m in range(3):
            coarse_buf[it, :, m] = coarse[m]
        coarse_arrived = [
            to_above(
                coarse_buf.at[it, layers - 1],
                coarse_halo.at[it, 0],
                coarse_send.at[it, 0],
                coarse_recv.at[it, 0],
            ),
            to_below(
                coarse_buf.at[it, 0],
                coarse_halo.at[it, 1],
                coarse_send.at[it, 1],
                coarse_recv.at[it, 1],
            ),
        ]
        if it + 1 < ITERS:
            for m in range(3):
                for p in range(4):
                    swept_buf[:, m, p] = swept[m][p]
            end_arrived = to_later(1, swept_buf.at[:, 2], end_in, end_send, end_recv)
            swept_arrived = [
                to_above(
                    swept_buf.at[layers - 1], swept_halo.at[0], swept_send.at[0], swept_recv.at[0]
                ),
                to_below(swept_buf.at[0], swept_halo.at[1], swept_send.at[1], swept_recv.at[1]),
            ]
        restricted = []
        for j in range(3):
            a, b, c, d = swept[j]
            edges = (down(c + d) + up(a + b)) + (right(b + d) + left(a + c))
            local = [jnp.tanh(swept[j][p]) - rate[p] * swept[j][p] for p in range(4)]
            restricted.append(
                0.25 * (diffusion * edges + total(local))
                + diffusion * (inner(coarse[j]) - 4.0 * coarse[j])
                + coarse_control
            )
        for arrived in coarse_arrived:
            arrived()
        restricted = [
            restricted[j]
            + diffusion * outer(coarse_halo[it, 0, j][None], coarse_halo[it, 1, j][None])
            for j in range(3)
        ]

        def offset_of(m):
            mixed = Q[m][0] * restricted[0] + Q[m][1] * restricted[1] + Q[m][2] * restricted[2]
            return scale[m] * (mixed + D[m] * coarse_rate * coarse[m])

        last = offset_of(2)
        offset_buf[it] = last
        offset_arrived = {
            d: to_later(
                d,
                offset_buf.at[it],
                offset_in.at[it, d - 1],
                offset_send.at[it, d - 1],
                offset_recv.at[it, d - 1],
            )
            for d in reversed(range(1, slices))
        }
        offset = [offset_of(0), offset_of(1), last]
        if it == 0:
            for d in range(1, slices):
                scale_arrived[d]()
        for d in range(1, slices):
            offset_arrived[d]()
        coarse_start = coarse_first
        for d in reversed(range(1, slices)):
            coarse_start = jnp.where(
                t >= d, scale_in[d - 1] * coarse_start + offset_in[it, d - 1], coarse_start
            )
        correction = [scale[m] * coarse_start + offset[m] - coarse[m] for m in range(3)]
        if it + 1 == ITERS:
            break
        for m in range(3):
            corr_buf[:, m] = correction[m]
        corr_arrived = [
            to_above(corr_buf.at[layers - 1], corr_halo.at[0], corr_send.at[0], corr_recv.at[0]),
            to_below(corr_buf.at[0], corr_halo.at[1], corr_send.at[1], corr_recv.at[1]),
        ]
        nodes = [[swept[m][p] + correction[m] for p in range(4)] for m in range(3)]
        forces = [force_inside(nodes[j]) for j in range(3)]
        end_arrived()
        ends = [end_in[:, p] for p in range(4)]
        shift = coarse_start - 0.25 * total(ends)
        start = [jnp.where(leading, initial[p], ends[p] + shift) for p in range(4)]
        for arrived in swept_arrived + corr_arrived:
            arrived()
        for j in range(3):
            for p in range(4):
                low = (swept_halo[0, j, p] + corr_halo[0, j])[None]
                high = (swept_halo[1, j, p] + corr_halo[1, j])[None]
                forces[j][p] = forces[j][p] + diffusion * outer(low, high)
        swept = [
            [
                (
                    start[p]
                    + (Q[m][0] * forces[0][p] + Q[m][1] * forces[1][p] + Q[m][2] * forces[2][p])
                    + D[m] * rate[p] * nodes[m][p]
                )
                * inverse[m][p]
                for p in range(4)
            ]
            for m in range(3)
        ]

    even_lane = lane3 % 2 == 0
    stores = []
    for m in range(3):
        node = [swept[m][p] + correction[m] for p in range(4)]
        for half, index in enumerate((low_index, high_index)):
            for px in range(2):
                out_buf[m, half, :, pl.ds(px, rows, stride=2), :] = jnp.where(
                    even_lane, take(node[2 * px], index), take(node[2 * px + 1], index)
                )
            store = pltpu.make_async_copy(
                out_buf.at[m, half],
                out_ref.at[0, m, :, :, pl.ds(half * width, width)],
                out_sem.at[m, half],
            )
            store.start()
            stores.append(store)
    for sent in pending:
        sent()
    for store in stores:
        store.wait()


def per_device(initial_state, start_guess, control, reaction_rate):
    slices = lax.axis_size("tm")
    slabs = lax.axis_size("gz")
    layers, depth_rows, columns = initial_state.shape
    rows, width = depth_rows // 2, columns // 2
    later = max(slices - 1, 1)
    vmem, dma = pltpu.VMEM, pltpu.SemaphoreType.DMA
    f32 = jnp.float32
    anywhere = pl.BlockSpec(memory_space=pl.ANY)
    return pl.pallas_call(
        functools.partial(kernel, slices, slabs),
        out_shape=jax.ShapeDtypeStruct((1, 3, layers, depth_rows, columns), f32),
        in_specs=[anywhere] * 4,
        out_specs=anywhere,
        scratch_shapes=[
            vmem((4, 2, layers, depth_rows, width), f32),
            vmem((2, 2, depth_rows, width), f32),
            vmem((layers, 3, 4, rows, width), f32),
            vmem((2, 3, 4, rows, width), f32),
            vmem((ITERS, layers, 3, rows, width), f32),
            vmem((ITERS, 2, 3, rows, width), f32),
            vmem((layers, 3, rows, width), f32),
            vmem((2, 3, rows, width), f32),
            vmem((layers, 4, rows, width), f32),
            vmem((layers, rows, width), f32),
            vmem((later, layers, rows, width), f32),
            vmem((ITERS, layers, rows, width), f32),
            vmem((ITERS, later, layers, rows, width), f32),
            vmem((3, 2, layers, depth_rows, width), f32),
            dma((4, 2)),
            dma((3, 2)),
            dma((2, 2)),
            dma((2, 2)),
            dma((2,)),
            dma((2,)),
            dma((ITERS, 2)),
            dma((ITERS, 2)),
            dma((2,)),
            dma((2,)),
            dma,
            dma,
            dma((later,)),
            dma((later,)),
            dma((ITERS, later)),
            dma((ITERS, later)),
        ],
        compiler_params=pltpu.CompilerParams(
            collective_id=0, has_side_effects=True, vmem_limit_bytes=32 * 1024 * 1024
        ),
    )(initial_state, start_guess, control, reaction_rate)


def solution(mesh):
    in_specs = (
        P(("groups", "gz"), None, None),
        P("tm", ("groups", "gz"), None, None),
        P("tm", ("groups", "gz"), None, None),
        P("tm", ("groups", "gz"), None, None),
    )
    out_specs = P("tm", None, ("groups", "gz"), None, None)
    return jax.shard_map(
        per_device, mesh=mesh, in_specs=in_specs, out_specs=out_specs, check_vma=False
    )
```

time: 79.3 us -> 23.1 us (0.29)
  the two profiles are of different devices: /device:TPU:30 before, /device:TPU:3 now
where the time goes in v1:
time: 23.1 us; the launch traced here: 22.8 us
  Pallas kernels  18.8 us (81%)
  local copies, waits for them, and re-layouts  4.04 us (17%)
    pallas_call x1, Pallas kernels, per_device(): pl.pallas_call(functools.partial(kernel, slices, slabs), out_shape=jax.Sh...  18.8 us
    unnamed x9, local copies, waits for them, and re-layouts  4.04 us

profile of v1, /device:TPU:3, one launch (start us, length us, event | category | flops | bytes accessed | tf_op | source)
XLA Modules:
  0.0 22.8 jit_solution(10027287385891976217)
XLA Ops:
  0.0 0.0 copy-start
  0.0 0.8 %copy-done = f32[4,16,256]{2,1,0:T(8,128)S(1)} copy-done((f32[4,16,256]{2,1,0:T(8,128)S(1)}, f32[4,16,256]{2,1,0:T(8,128)}, u32[]{:S(2)}) %copy-start) | copy-done | bytes 65560
  0.8 0.0 copy-start.1
  0.8 0.8 %copy-done.1 = f32[1,4,16,256]{3,2,1,0:T(8,128)S(1)} copy-done((f32[1,4,16,256]{3,2,1,0:T(8,128)S(1)}, f32[1,4,16,256]{3,2,1,0:T(8,128)}, u32[]{:S(2)}) %copy-start.1) | copy-done | bytes 65560
  1.7 0.0 copy-start.2
  1.7 0.8 %copy-done.2 = f32[1,4,16,256]{3,2,1,0:T(8,128)S(1)} copy-done((f32[1,4,16,256]{3,2,1,0:T(8,128)S(1)}, f32[1,4,16,256]{3,2,1,0:T(8,128)}, u32[]{:S(2)}) %copy-start.2) | copy-done | bytes 65560
  2.5 0.0 copy-start.3
  2.5 0.8 %copy-done.3 = f32[1,4,16,256]{3,2,1,0:T(8,128)S(1)} copy-done((f32[1,4,16,256]{3,2,1,0:T(8,128)S(1)}, f32[1,4,16,256]{3,2,1,0:T(8,128)}, u32[]{:S(2)}) %copy-start.3) | copy-done | bytes 65560
  3.4 18.8 %shard_map.46 = f32[1,3,4,16,256]{4,3,2,1,0:T(8,128)S(1)} custom-call(f32[4,16,256]{2,1,0:T(8,128)S(1)} %copy-done, f32[1,4,16,256]{3,2,1,0:T(8,128)S(1)} %copy-done.1, f32[1,4,16,256]{3,2,1,0:T(8,128)S(1)} %copy-done.2, f32[1,4,16,256]{3,2,1,0:T(8,128)S(1)} %copy-done.3), custom_call_target="tpu_custom_call" | custom-call | tf_op jit(solution)/shard_map/pallas_call | solution.py:442
  22.1 0.7 %copy.6 = f32[1,3,4,16,256]{4,3,2,1,0:T(8,128)} copy(f32[1,3,4,16,256]{4,3,2,1,0:T(8,128)S(1)} %shard_map.46) | data formatting | bytes 393216
Async XLA Ops:
  0.0 0.8 %copy-start = (f32[4,16,256]{2,1,0:T(8,128)S(1)}, f32[4,16,256]{2,1,0:T(8,128)}, u32[]{:S(2)}) copy-start(f32[4,16,256]{2,1,0:T(8,128)} %init_ref.1) | copy-start | bytes 196612
  0.8 0.8 %copy-start.1 = (f32[1,4,16,256]{3,2,1,0:T(8,128)S(1)}, f32[1,4,16,256]{3,2,1,0:T(8,128)}, u32[]{:S(2)}) copy-start(f32[1,4,16,256]{3,2,1,0:T(8,128)} %guess_ref.1) | copy-start | bytes 196612
  1.7 0.8 %copy-start.2 = (f32[1,4,16,256]{3,2,1,0:T(8,128)S(1)}, f32[1,4,16,256]{3,2,1,0:T(8,128)}, u32[]{:S(2)}) copy-start(f32[1,4,16,256]{3,2,1,0:T(8,128)} %control_ref.1) | copy-start | bytes 196612
  2.5 0.8 %copy-start.3 = (f32[1,4,16,256]{3,2,1,0:T(8,128)S(1)}, f32[1,4,16,256]{3,2,1,0:T(8,128)}, u32[]{:S(2)}) copy-start(f32[1,4,16,256]{3,2,1,0:T(8,128)} %rate_ref.1) | copy-start | bytes 196612

commit v2 on v0

v2 whole, which is shorter than its diff:
```python
import functools
import math
import types

import jax
import jax.numpy as jnp
from jax import lax
from jax.experimental import pallas as pl
from jax.experimental.pallas import tpu as pltpu
from jax.sharding import PartitionSpec as P

ITERS = 2

root_six = math.sqrt(6.0)
Q = (
    (
        (88.0 - 7.0 * root_six) / 360.0,
        (296.0 - 169.0 * root_six) / 1800.0,
        (-2.0 + 3.0 * root_six) / 225.0,
    ),
    (
        (296.0 + 169.0 * root_six) / 1800.0,
        (88.0 + 7.0 * root_six) / 360.0,
        (-2.0 - 3.0 * root_six) / 225.0,
    ),
    ((16.0 - root_six) / 36.0, (16.0 + root_six) / 36.0, 1.0 / 9.0),
)
D = tuple(Q[m][m] for m in range(3))
ROW = tuple(sum(Q[m]) for m in range(3))
diffusion = 0.1
VMEM_LIMIT = 60 * 1024 * 1024
MESH = pl.DeviceIdType.MESH


def kernel(slices, slabs, init_ref, guess_ref, control_ref, rate_ref, out_ref, r):
    t = lax.axis_index("tm")
    z = lax.axis_index("gz")
    layers, depth_rows, width = r.raw.shape[2:]
    rows = depth_rows // 2
    has_above = z < slabs - 1
    has_below = z > 0
    leading = t == 0

    sources = (guess_ref.at[0], rate_ref.at[0], control_ref.at[0], init_ref)
    halves = [pl.ds(half * width, width) for half in range(2)]
    loads = [
        [
            pltpu.make_async_copy(
                source.at[:, :, halves[half]], r.raw.at[field, half], r.in_sem.at[field, half]
            )
            for half in range(2)
        ]
        for field, source in enumerate(sources)
    ]
    for pair in loads:
        for load in pair:
            load.start()

    barrier = pltpu.get_barrier_semaphore()

    def greet(condition, device):
        @pl.when(condition)
        def _():
            pl.semaphore_signal(barrier, inc=1, device_id=device, device_id_type=MESH)

    greet(has_above, {"gz": z + 1})
    greet(has_below, {"gz": z - 1})
    for d in range(1, slices):
        greet(t >= d, {"tm": t - d})
        greet((t >= d) & has_above, {"tm": t - d, "gz": z + 1})
        greet((t >= d) & has_below, {"tm": t - d, "gz": z - 1})
    beside = has_above.astype(jnp.int32) + has_below.astype(jnp.int32)

    @pl.when(z == 0)
    def _():
        r.halo[:, :, 0] = jnp.zeros_like(r.halo[:, :, 0])

    @pl.when(z == slabs - 1)
    def _():
        r.halo[:, :, 1] = jnp.zeros_like(r.halo[:, :, 1])

    pl.semaphore_wait(barrier, beside + (slices - 1 - t) * (1 + beside))

    pending = []

    def remote(src, dst, send, recv, device, sends, receives):
        copy = pltpu.make_async_remote_copy(
            src_ref=src,
            dst_ref=dst,
            send_sem=send,
            recv_sem=recv,
            device_id=device,
            device_id_type=MESH,
        )

        @pl.when(sends)
        def _():
            copy.start()

        def sent():
            @pl.when(sends)
            def _():
                copy.wait_send()

        def arrived():
            @pl.when(receives)
            def _():
                copy.wait_recv()

        pending.append(sent)
        return arrived

    def beside_copies(sources, dst, send, recv, d=0, only=None):
        sends = t + d < slices
        receives = t >= d
        if only is not None:
            sends, receives = only
        return [
            remote(
                sources[side],
                dst(side),
                send.at[side],
                recv.at[side],
                {"tm": t + d, "gz": z + step},
                sends & here,
                receives & there,
            )
            for side, step, here, there in (
                (0, 1, has_above, has_below),
                (1, -1, has_below, has_above),
            )
        ]

    def later_copy(d, src, dst, send, recv, only=None):
        sends, receives = (t + d < slices, t >= d) if only is None else only
        return remote(src, dst, send, recv, {"tm": t + d}, sends, receives)

    always = (t >= 0, t >= 0)
    first_only = (leading, leading)

    def halo_copies(field, source, low_ring, high_ring, index, only):
        count = high_ring - low_ring + 1
        out = []
        for half in range(2):
            up = source.at[pl.ds(layers - high_ring, count), :, halves[half]]
            down = source.at[pl.ds(low_ring - 1, count), :, halves[half]]
            starts = (3 - high_ring, low_ring - 1)
            out += beside_copies(
                (up, down),
                lambda side: r.halo.at[field, half, side, pl.ds(starts[side], count)],
                r.halo_send.at[index, half],
                r.halo_recv.at[index, half],
                only=only,
            )
        return out

    guess_src, rate_src, control_src, init_src = sources
    near = halo_copies(0, guess_src, 1, 2, 0, always)
    near += halo_copies(1, rate_src, 1, 1, 1, always)
    near += halo_copies(2, control_src, 1, 1, 2, always)
    near += halo_copies(3, init_src, 1, 1, 3, first_only)
    far = halo_copies(1, rate_src, 2, 2, 4, always)
    far += halo_copies(0, guess_src, 3, 3, 5, always)
    far += halo_copies(2, control_src, 2, 2, 6, always)
    far += halo_copies(3, init_src, 2, 2, 7, first_only)

    lane = lax.broadcasted_iota(jnp.int32, (layers * rows, width), 1)
    lane3 = lax.broadcasted_iota(jnp.int32, (layers, rows, width), 2)
    row3 = lax.broadcasted_iota(jnp.int32, (layers, rows, width), 1)
    even_index = (2 * lane) % width
    odd_index = even_index + 1
    low_index = lane // 2
    high_index = low_index + width // 2

    def take(array, index):
        flat = array.reshape(-1, width)
        picked = jnp.take_along_axis(
            flat, index[: flat.shape[0]], axis=1, mode="promise_in_bounds"
        )
        return picked.reshape(array.shape)

    def split(low, high):
        front = lane3[: low.shape[0]] < width // 2
        return [
            jnp.where(front, take(low, index), take(high, index))
            for index in (even_index, odd_index)
        ]

    def core_of(field):
        for load in loads[field]:
            load.wait()
        out = []
        for px in range(2):
            low = r.raw[field, 0, :, pl.ds(px, rows, stride=2), :]
            high = r.raw[field, 1, :, pl.ds(px, rows, stride=2), :]
            out += split(low, high)
        return out

    def rim_of(field, ring):
        out = []
        for px in range(2):
            low, high = [
                jnp.concatenate(
                    [
                        r.halo[field, half, side, index, pl.ds(px, rows, stride=2), :][None]
                        for side, index in ((0, 3 - ring), (1, ring - 1))
                    ],
                    0,
                )
                for half in range(2)
            ]
            out += split(low, high)
        return out

    rim_side = lax.broadcasted_iota(jnp.int32, (2, rows, width), 0)
    rim_inside = ((rim_side == 0) & has_below) | ((rim_side == 1) & has_above)

    def inside(v):
        return jnp.where(rim_inside, v, 0.0)

    def down(v):
        return jnp.where(row3[: v.shape[0]] == 0, 0.0, pltpu.roll(v, 1, 1))

    def up(v):
        return jnp.where(row3[: v.shape[0]] == rows - 1, 0.0, pltpu.roll(v, rows - 1, 1))

    def right(v):
        return jnp.where(lane3[: v.shape[0]] == 0, 0.0, pltpu.roll(v, 1, 2))

    def left(v):
        return jnp.where(lane3[: v.shape[0]] == width - 1, 0.0, pltpu.roll(v, width - 1, 2))

    def planar(v):
        a, b, c, d = v
        return [
            (c + down(c)) + (b + right(b)),
            (d + down(d)) + (a + left(a)),
            (a + up(a)) + (d + right(d)),
            (b + up(b)) + (c + left(c)),
        ]

    def inner(v):
        below = jnp.concatenate([jnp.zeros_like(v[:1]), v[:-1]], 0)
        above = jnp.concatenate([v[1:], jnp.zeros_like(v[:1])], 0)
        return below + above

    def outer(rim):
        gap = jnp.zeros((layers - 2, rows, width), jnp.float32)
        return jnp.concatenate([rim[:1], gap, rim[1:]], 0)

    def ends_of(v):
        return jnp.concatenate([v[:1], v[layers - 1 :]], 0)

    def total(v):
        return (v[0] + v[1]) + (v[2] + v[3])

    def force_of(v, depth, control, rate):
        flat = planar(v)
        return [
            diffusion * (flat[p] + depth[p] - 6.0 * v[p])
            + jnp.tanh(v[p])
            + control[p]
            - rate[p] * v[p]
            for p in range(4)
        ]

    def sweep_of(start, integral, rate, nodes, inverse):
        return [
            [
                (start[p] + integral[m][p] + D[m] * rate[p] * nodes[m][p]) * inverse[m][p]
                for p in range(4)
            ]
            for m in range(3)
        ]

    def inverse_of(rate):
        return [[1.0 / (1.0 + D[m] * rate[p]) for p in range(4)] for m in range(3)]

    def scale_of(coarse_rate):
        return [1.0 / (1.0 + D[m] * coarse_rate) for m in range(3)]

    def first_sweep(start, force, rate, guess, inverse):
        integral = [[ROW[m] * force[p] for p in range(4)] for m in range(3)]
        return sweep_of(start, integral, rate, [guess] * 3, inverse)

    def mix(m, v):
        return Q[m][0] * v[0] + Q[m][1] * v[1] + Q[m][2] * v[2]

    guess = core_of(0)
    rate = core_of(1)
    coarse_rate = 0.25 * total(rate)
    scale = scale_of(coarse_rate)
    r.scale_buf[...] = scale[2]
    scale_arrived = []
    for d in range(1, slices):
        only = ((t > 0) & (t + d < slices), t > d)
        scale_arrived.append(
            later_copy(
                d,
                r.scale_buf,
                r.scale_in.at[d - 1],
                r.scale_send.at[d - 1],
                r.scale_recv.at[d - 1],
                only,
            )
        )
        scale_arrived += beside_copies(
            (r.scale_buf.at[pl.ds(layers - 2, 2)], r.scale_buf.at[pl.ds(0, 2)]),
            lambda side: r.scale_rim_in.at[d - 1, side],
            r.scale_rim_send.at[d - 1],
            r.scale_rim_recv.at[d - 1],
            d,
            only,
        )
    control = core_of(2)
    initial = core_of(3)
    coarse_first = 0.25 * total(initial)
    coarse_control = 0.25 * total(control)
    start = [jnp.where(leading, initial[p], guess[p]) for p in range(4)]
    inverse = inverse_of(rate)

    force = force_of(guess, [inner(v) for v in guess], control, rate)
    for arrived in near:
        arrived()
    guess1, guess2 = rim_of(0, 1), rim_of(0, 2)
    rate1, control1, initial1 = rim_of(1, 1), rim_of(2, 1), rim_of(3, 1)
    force = [force[p] + diffusion * outer(guess1[p]) for p in range(4)]
    swept = first_sweep(start, force, rate, guess, inverse)
    inverse1 = inverse_of(rate1)
    start1 = [jnp.where(leading, initial1[p], guess1[p]) for p in range(4)]
    force1 = force_of(guess1, [guess2[p] + ends_of(guess[p]) for p in range(4)], control1, rate1)
    swept1 = first_sweep(start1, force1, rate1, guess1, inverse1)
    swept1 = [[inside(v) for v in node] for node in swept1]

    def offsets_of(swept, coarse, coarse_rim):
        restricted = []
        for j in range(3):
            a, b, c, d = swept[j]
            edges = (down(c + d) + up(a + b)) + (right(b + d) + left(a + c))
            local = [jnp.tanh(swept[j][p]) - rate[p] * swept[j][p] for p in range(4)]
            restricted.append(
                0.25 * (diffusion * edges + total(local))
                + diffusion * (inner(coarse[j]) - 4.0 * coarse[j] + outer(coarse_rim[j]))
                + coarse_control
            )
        return [
            scale[m] * (mix(m, restricted) + D[m] * coarse_rate * coarse[m]) for m in (0, 1, 2)
        ]

    def send_offset(it, last):
        r.offset_buf[it] = jnp.where(leading, scale[2] * coarse_first + last, last)
        return [
            later_copy(
                d,
                r.offset_buf.at[it],
                r.offset_in.at[it, d - 1],
                r.offset_send.at[it, d - 1],
                r.offset_recv.at[it, d - 1],
            )
            for d in reversed(range(1, slices))
        ]

    def chain(first, scales, offsets):
        current = first
        for d in reversed(range(1, slices)):
            moved = scales(d) * current + offsets(d)
            current = jnp.where(t > d, moved, jnp.where(t == d, offsets(d), current))
        return current

    coarse = [0.25 * total(swept[m]) for m in range(3)]
    coarse1 = [0.25 * total(swept1[m]) for m in range(3)]
    offset = offsets_of(swept, coarse, coarse1)
    offset_arrived = send_offset(0, offset[2])
    for d in range(1, slices):
        offset_arrived += beside_copies(
            (r.offset_buf.at[0, pl.ds(layers - 2, 2)], r.offset_buf.at[0, pl.ds(0, 2)]),
            lambda side: r.offset_rim_in.at[d - 1, side],
            r.offset_rim_send.at[d - 1],
            r.offset_rim_recv.at[d - 1],
            d,
        )
    for m in range(3):
        r.own_buf[:, m] = offset[m]
    own_arrived = beside_copies(
        (r.own_buf.at[pl.ds(layers - 2, 2)], r.own_buf.at[pl.ds(0, 2)]),
        lambda side: r.own_rim.at[side],
        r.own_send,
        r.own_recv,
    )
    for p in range(4):
        r.end_buf[pl.ds(1, layers), p] = swept[2][p]
        r.end_buf[0, p] = swept1[2][p][0]
        r.end_buf[layers + 1, p] = swept1[2][p][1]
    end_arrived = later_copy(1, r.end_buf, r.end_in, r.end_send, r.end_recv)

    for arrived in far:
        arrived()
    guess3 = rim_of(0, 3)
    rate2, control2, initial2 = rim_of(1, 2), rim_of(2, 2), rim_of(3, 2)
    start2 = [jnp.where(leading, initial2[p], guess2[p]) for p in range(4)]
    force2 = force_of(guess2, [guess3[p] + guess1[p] for p in range(4)], control2, rate2)
    swept2 = first_sweep(start2, force2, rate2, guess2, inverse_of(rate2))
    coarse2 = [0.25 * total(swept2[m]) for m in range(3)]
    scale1, scale2 = scale_of(0.25 * total(rate1)), scale_of(0.25 * total(rate2))

    for arrived in scale_arrived + offset_arrived:
        arrived()
    coarse_start = chain(
        coarse_first, lambda d: r.scale_in[d - 1], lambda d: r.offset_in[0, d - 1]
    )

    def ring(ref, k):
        return jnp.concatenate([ref[0, 2 - k][None], ref[1, k - 1][None]], 0)

    start_rim = [
        chain(
            0.25 * total(initial_ring),
            lambda d: ring(r.scale_rim_in.at[d - 1], k),
            lambda d: ring(r.offset_rim_in.at[d - 1], k),
        )
        for k, initial_ring in ((1, initial1), (2, initial2))
    ]
    correction = [scale[m] * coarse_start + offset[m] - coarse[m] for m in range(3)]
    nodes = [[swept[m][p] + correction[m] for p in range(4)] for m in range(3)]
    for arrived in own_arrived:
        arrived()

    def rim_nodes(k, scales, coarses, sweeps):
        own = ring(r.own_rim, k)
        out = []
        for m in range(3):
            corrected = scales[m] * start_rim[k - 1] + own[:, m] - coarses[m]
            out.append([inside(sweeps[m][p] + corrected) for p in range(4)])
        return out

    nodes1 = rim_nodes(1, scale1, coarse1, swept1)
    nodes2 = rim_nodes(2, scale2, coarse2, swept2)
    forces = [
        force_of(
            nodes[j], [inner(nodes[j][p]) + outer(nodes1[j][p]) for p in range(4)], control, rate
        )
        for j in range(3)
    ]
    forces1 = [
        force_of(
            nodes1[j],
            [nodes2[j][p] + ends_of(nodes[j][p]) for p in range(4)],
            control1,
            rate1,
        )
        for j in range(3)
    ]
    integral = [[mix(m, [forces[j][p] for j in range(3)]) for p in range(4)] for m in range(3)]
    integral1 = [[mix(m, [forces1[j][p] for j in range(3)]) for p in range(4)] for m in range(3)]
    end_arrived()
    ends = [r.end_in[pl.ds(1, layers), p] for p in range(4)]
    ends1 = [
        jnp.concatenate([r.end_in[0, p][None], r.end_in[layers + 1, p][None]], 0) for p in range(4)
    ]
    shift = coarse_start - 0.25 * total(ends)
    shift1 = start_rim[0] - 0.25 * total(ends1)
    start = [jnp.where(leading, initial[p], ends[p] + shift) for p in range(4)]
    start1 = [jnp.where(leading, initial1[p], ends1[p] + shift1) for p in range(4)]
    swept = sweep_of(start, integral, rate, nodes, inverse)
    swept1 = sweep_of(start1, integral1, rate1, nodes1, inverse1)

    coarse = [0.25 * total(swept[m]) for m in range(3)]
    coarse1 = [inside(0.25 * total(swept1[m])) for m in range(3)]
    offset = offsets_of(swept, coarse, coarse1)
    for arrived in send_offset(1, offset[2]):
        arrived()
    coarse_start = chain(
        coarse_first, lambda d: r.scale_in[d - 1], lambda d: r.offset_in[1, d - 1]
    )
    correction = [scale[m] * coarse_start + offset[m] - coarse[m] for m in range(3)]

    even_lane = lane3 % 2 == 0
    stores = []
    for m in range(3):
        node = [swept[m][p] + correction[m] for p in range(4)]
        for half, index in enumerate((low_index, high_index)):
            for px in range(2):
                r.out_buf[m, half, :, pl.ds(px, rows, stride=2), :] = jnp.where(
                    even_lane, take(node[2 * px], index), take(node[2 * px + 1], index)
                )
            store = pltpu.make_async_copy(
                r.out_buf.at[m, half],
                out_ref.at[0, m, :, :, halves[half]],
                r.out_sem.at[m, half],
            )
            store.start()
            stores.append(store)
    for sent in pending:
        sent()
    for store in stores:
        store.wait()


def per_device(initial_state, start_guess, control, reaction_rate):
    slices = lax.axis_size("tm")
    slabs = lax.axis_size("gz")
    layers, depth_rows, columns = initial_state.shape
    rows, width = depth_rows // 2, columns // 2
    later = slices - 1
    vmem = functools.partial(pltpu.VMEM, dtype=jnp.float32)
    dma = pltpu.SemaphoreType.DMA
    coarse = (layers, rows, width)
    scratch = dict(
        raw=vmem((4, 2, layers, depth_rows, width)),
        halo=vmem((4, 2, 2, 3, depth_rows, width)),
        scale_buf=vmem(coarse),
        scale_in=vmem((later,) + coarse),
        scale_rim_in=vmem((later, 2, 2, rows, width)),
        offset_buf=vmem((ITERS,) + coarse),
        offset_in=vmem((ITERS, later) + coarse),
        offset_rim_in=vmem((later, 2, 2, rows, width)),
        own_buf=vmem((layers, 3, rows, width)),
        own_rim=vmem((2, 2, 3, rows, width)),
        end_buf=vmem((layers + 2, 4, rows, width)),
        end_in=vmem((layers + 2, 4, rows, width)),
        out_buf=vmem((3, 2, layers, depth_rows, width)),
        in_sem=dma((4, 2)),
        out_sem=dma((3, 2)),
        halo_send=dma((8, 2, 2)),
        halo_recv=dma((8, 2, 2)),
        scale_send=dma((later,)),
        scale_recv=dma((later,)),
        scale_rim_send=dma((later, 2)),
        scale_rim_recv=dma((later, 2)),
        offset_send=dma((ITERS, later)),
        offset_recv=dma((ITERS, later)),
        offset_rim_send=dma((later, 2)),
        offset_rim_recv=dma((later, 2)),
        own_send=dma((2,)),
        own_recv=dma((2,)),
        end_send=dma,
        end_recv=dma,
    )
    names = list(scratch)

    def body(*refs):
        kernel(slices, slabs, *refs[:5], types.SimpleNamespace(**dict(zip(names, refs[5:]))))

    return pl.pallas_call(
        body,
        out_shape=jax.ShapeDtypeStruct((1, 3, layers, depth_rows, columns), jnp.float32),
        in_specs=[pl.BlockSpec(memory_space=pl.ANY)] * 4,
        out_specs=pl.BlockSpec(memory_space=pl.ANY),
        scratch_shapes=list(scratch.values()),
        compiler_params=pltpu.CompilerParams(
            collective_id=0, has_side_effects=True, vmem_limit_bytes=VMEM_LIMIT
        ),
    )(initial_state, start_guess, control, reaction_rate)


def solution(mesh):
    in_specs = (
        P(("groups", "gz"), None, None),
        P("tm", ("groups", "gz"), None, None),
        P("tm", ("groups", "gz"), None, None),
        P("tm", ("groups", "gz"), None, None),
    )
    out_specs = P("tm", None, ("groups", "gz"), None, None)
    return jax.shard_map(
        per_device, mesh=mesh, in_specs=in_specs, out_specs=out_specs, check_vma=False
    )
```

time: 79.3 us -> 18 us (0.23)
  the two profiles are of different devices: /device:TPU:30 before, /device:TPU:3 now
where the time goes in v2:
time: 18 us; the launch traced here: 17.7 us
  Pallas kernels  16.1 us (89%)
  local copies, waits for them, and re-layouts  1.62 us (9%)
    pallas_call x1, Pallas kernels, per_device(): pl.pallas_call(body, out_shape=jax.ShapeDtypeStruct((1, 3, layers, depth_...  16.1 us
    unnamed x1, local copies, waits for them, and re-layouts  1.62 us

profile of v2, /device:TPU:3, one launch (start us, length us, event | category | flops | bytes accessed | tf_op | source)
XLA Modules:
  0.0 17.7 jit_solution(11276565528709944351)
XLA Ops:
  0.0 16.1 %shard_map.46 = f32[1,3,4,16,256]{4,3,2,1,0:T(8,128)} custom-call(f32[4,16,256]{2,1,0:T(8,128)} %refs_0_.1, f32[1,4,16,256]{3,2,1,0:T(8,128)} %refs_1_.1, f32[1,4,16,256]{3,2,1,0:T(8,128)} %refs_2_.1, f32[1,4,16,256]{3,2,1,0:T(8,128)} %refs_3_.1), custom_call_target="tpu_custom_call" | custom-call | tf_op jit(solution)/shard_map/pallas_call | solution.py:544
  16.1 1.6 %copy.6 = f32[1,3,4,16,256]{4,3,2,1,0:T(8,128)} copy(f32[1,3,4,16,256]{4,3,2,1,0:T(8,128)} %shard_map.46) | data formatting | bytes 393216

commit v3 on v2

--- a/solution.py
+++ b/solution.py
@@ -73,11 +73,11 @@
 
     @pl.when(z == 0)
     def _():
-        r.halo[:, :, 0] = jnp.zeros_like(r.halo[:, :, 0])
+        r.halo[:, 0] = jnp.zeros_like(r.halo[:, 0])
 
     @pl.when(z == slabs - 1)
     def _():
-        r.halo[:, :, 1] = jnp.zeros_like(r.halo[:, :, 1])
+        r.halo[:, 1] = jnp.zeros_like(r.halo[:, 1])
 
     pl.semaphore_wait(barrier, beside + (slices - 1 - t) * (1 + beside))
 
@@ -140,19 +140,14 @@
 
     def halo_copies(field, source, low_ring, high_ring, index, only):
         count = high_ring - low_ring + 1
-        out = []
-        for half in range(2):
-            up = source.at[pl.ds(layers - high_ring, count), :, halves[half]]
-            down = source.at[pl.ds(low_ring - 1, count), :, halves[half]]
-            starts = (3 - high_ring, low_ring - 1)
-            out += beside_copies(
-                (up, down),
-                lambda side: r.halo.at[field, half, side, pl.ds(starts[side], count)],
-                r.halo_send.at[index, half],
-                r.halo_recv.at[index, half],
-                only=only,
-            )
-        return out
+        starts = (3 - high_ring, low_ring - 1)
+        return beside_copies(
+            (source.at[pl.ds(layers - high_ring, count)], source.at[pl.ds(low_ring - 1, count)]),
+            lambda side: r.halo.at[field, side, pl.ds(starts[side], count)],
+            r.halo_send.at[index],
+            r.halo_recv.at[index],
+            only=only,
+        )
 
     guess_src, rate_src, control_src, init_src = sources
     near = halo_copies(0, guess_src, 1, 2, 0, always)
@@ -197,12 +192,15 @@
         return out
 
     def rim_of(field, ring):
+        for side, index in ((0, 3 - ring), (1, ring - 1)):
+            for half in range(2):
+                r.rim[field, half, side, index] = r.halo[field, side, index, :, halves[half]]
         out = []
         for px in range(2):
             low, high = [
                 jnp.concatenate(
                     [
-                        r.halo[field, half, side, index, pl.ds(px, rows, stride=2), :][None]
+                        r.rim[field, half, side, index, pl.ds(px, rows, stride=2), :][None]
                         for side, index in ((0, 3 - ring), (1, ring - 1))
                     ],
                     0,
@@ -291,10 +289,10 @@
     coarse_rate = 0.25 * total(rate)
     scale = scale_of(coarse_rate)
     r.scale_buf[...] = scale[2]
-    scale_arrived = []
+    core_arrived, rim_arrived = [], []
     for d in range(1, slices):
         only = ((t > 0) & (t + d < slices), t > d)
-        scale_arrived.append(
+        core_arrived.append(
             later_copy(
                 d,
                 r.scale_buf,
@@ -304,7 +302,7 @@
                 only,
             )
         )
-        scale_arrived += beside_copies(
+        rim_arrived += beside_copies(
             (r.scale_buf.at[pl.ds(layers - 2, 2)], r.scale_buf.at[pl.ds(0, 2)]),
             lambda side: r.scale_rim_in.at[d - 1, side],
             r.scale_rim_send.at[d - 1],
@@ -370,9 +368,9 @@
     coarse = [0.25 * total(swept[m]) for m in range(3)]
     coarse1 = [0.25 * total(swept1[m]) for m in range(3)]
     offset = offsets_of(swept, coarse, coarse1)
-    offset_arrived = send_offset(0, offset[2])
+    core_arrived += send_offset(0, offset[2])
     for d in range(1, slices):
-        offset_arrived += beside_copies(
+        rim_arrived += beside_copies(
             (r.offset_buf.at[0, pl.ds(layers - 2, 2)], r.offset_buf.at[0, pl.ds(0, 2)]),
             lambda side: r.offset_rim_in.at[d - 1, side],
             r.offset_rim_send.at[d - 1],
@@ -403,11 +401,20 @@
     coarse2 = [0.25 * total(swept2[m]) for m in range(3)]
     scale1, scale2 = scale_of(0.25 * total(rate1)), scale_of(0.25 * total(rate2))
 
-    for arrived in scale_arrived + offset_arrived:
+    for arrived in core_arrived:
         arrived()
     coarse_start = chain(
         coarse_first, lambda d: r.scale_in[d - 1], lambda d: r.offset_in[0, d - 1]
     )
+
+    correction = [scale[m] * coarse_start + offset[m] - coarse[m] for m in range(3)]
+    nodes = [[swept[m][p] + correction[m] for p in range(4)] for m in range(3)]
+    forces = [
+        force_of(nodes[j], [inner(nodes[j][p]) for p in range(4)], control, rate)
+        for j in range(3)
+    ]
+    for arrived in rim_arrived + own_arrived:
+        arrived()
 
     def ring(ref, k):
         return jnp.concatenate([ref[0, 2 - k][None], ref[1, k - 1][None]], 0)
@@ -420,10 +427,6 @@
         )
         for k, initial_ring in ((1, initial1), (2, initial2))
     ]
-    correction = [scale[m] * coarse_start + offset[m] - coarse[m] for m in range(3)]
-    nodes = [[swept[m][p] + correction[m] for p in range(4)] for m in range(3)]
-    for arrived in own_arrived:
-        arrived()
 
     def rim_nodes(k, scales, coarses, sweeps):
         own = ring(r.own_rim, k)
@@ -436,10 +439,7 @@
     nodes1 = rim_nodes(1, scale1, coarse1, swept1)
     nodes2 = rim_nodes(2, scale2, coarse2, swept2)
     forces = [
-        force_of(
-            nodes[j], [inner(nodes[j][p]) + outer(nodes1[j][p]) for p in range(4)], control, rate
-        )
-        for j in range(3)
+        [forces[j][p] + diffusion * outer(nodes1[j][p]) for p in range(4)] for j in range(3)
     ]
     forces1 = [
         force_of(
@@ -507,7 +507,8 @@
     coarse = (layers, rows, width)
     scratch = dict(
         raw=vmem((4, 2, layers, depth_rows, width)),
-        halo=vmem((4, 2, 2, 3, depth_rows, width)),
+        halo=vmem((4, 2, 3, depth_rows, columns)),
+        rim=vmem((4, 2, 2, 3, depth_rows, width)),
         scale_buf=vmem(coarse),
         scale_in=vmem((later,) + coarse),
         scale_rim_in=vmem((later, 2, 2, rows, width)),
@@ -521,8 +522,8 @@
         out_buf=vmem((3, 2, layers, depth_rows, width)),
         in_sem=dma((4, 2)),
         out_sem=dma((3, 2)),
-        halo_send=dma((8, 2, 2)),
-        halo_recv=dma((8, 2, 2)),
+        halo_send=dma((8, 2)),
+        halo_recv=dma((8, 2)),
         scale_send=dma((later,)),
         scale_recv=dma((later,)),
         scale_rim_send=dma((later, 2)),

time: 18 us -> 17.7 us (0.983)
  Pallas kernels: 16.1 us -> 15.7 us
    pallas_call x1, Pallas kernels: 16.1 us -> 15.7 us  [per_device(): pl.pallas_call(body, out_shape=jax.ShapeDtypeStruct((1, 3, layers, depth_...]
where the time goes in v3:
time: 17.7 us; the launch traced here: 17.3 us
  Pallas kernels  15.7 us (89%)
  local copies, waits for them, and re-layouts  1.62 us (9%)
    pallas_call x1, Pallas kernels, per_device(): pl.pallas_call(body, out_shape=jax.ShapeDtypeStruct((1, 3, layers, depth_...  15.7 us
    unnamed x1, local copies, waits for them, and re-layouts  1.62 us

profile of v3, /device:TPU:3, one launch (start us, length us, event | category | flops | bytes accessed | tf_op | source)
XLA Modules:
  0.0 17.3 jit_solution(5830787034824773495)
XLA Ops:
  0.0 15.7 %shard_map.46 = f32[1,3,4,16,256]{4,3,2,1,0:T(8,128)} custom-call(f32[4,16,256]{2,1,0:T(8,128)} %refs_0_.1, f32[1,4,16,256]{3,2,1,0:T(8,128)} %refs_1_.1, f32[1,4,16,256]{3,2,1,0:T(8,128)} %refs_2_.1, f32[1,4,16,256]{3,2,1,0:T(8,128)} %refs_3_.1), custom_call_target="tpu_custom_call" | custom-call | tf_op jit(solution)/shard_map/pallas_call | solution.py:545
  15.7 1.6 %copy.6 = f32[1,3,4,16,256]{4,3,2,1,0:T(8,128)} copy(f32[1,3,4,16,256]{4,3,2,1,0:T(8,128)} %shard_map.46) | data formatting | bytes 393216

commit v4 on v3

--- a/solution.py
+++ b/solution.py
@@ -67,8 +67,6 @@
     greet(has_below, {"gz": z - 1})
     for d in range(1, slices):
         greet(t >= d, {"tm": t - d})
-        greet((t >= d) & has_above, {"tm": t - d, "gz": z + 1})
-        greet((t >= d) & has_below, {"tm": t - d, "gz": z - 1})
     beside = has_above.astype(jnp.int32) + has_below.astype(jnp.int32)
 
     @pl.when(z == 0)
@@ -79,7 +77,7 @@
     def _():
         r.halo[:, 1] = jnp.zeros_like(r.halo[:, 1])
 
-    pl.semaphore_wait(barrier, beside + (slices - 1 - t) * (1 + beside))
+    pl.semaphore_wait(barrier, beside + (slices - 1 - t))
 
     pending = []
 
@@ -140,7 +138,7 @@
 
     def halo_copies(field, source, low_ring, high_ring, index, only):
         count = high_ring - low_ring + 1
-        starts = (3 - high_ring, low_ring - 1)
+        starts = (4 - high_ring, low_ring - 1)
         return beside_copies(
             (source.at[pl.ds(layers - high_ring, count)], source.at[pl.ds(low_ring - 1, count)]),
             lambda side: r.halo.at[field, side, pl.ds(starts[side], count)],
@@ -154,10 +152,10 @@
     near += halo_copies(1, rate_src, 1, 1, 1, always)
     near += halo_copies(2, control_src, 1, 1, 2, always)
     near += halo_copies(3, init_src, 1, 1, 3, first_only)
-    far = halo_copies(1, rate_src, 2, 2, 4, always)
-    far += halo_copies(0, guess_src, 3, 3, 5, always)
-    far += halo_copies(2, control_src, 2, 2, 6, always)
-    far += halo_copies(3, init_src, 2, 2, 7, first_only)
+    far = halo_copies(1, rate_src, 2, 3, 4, always)
+    far += halo_copies(0, guess_src, 3, 4, 5, always)
+    far += halo_copies(2, control_src, 2, 3, 6, always)
+    far += halo_copies(3, init_src, 2, 3, 7, first_only)
 
     lane = lax.broadcasted_iota(jnp.int32, (layers * rows, width), 1)
     lane3 = lax.broadcasted_iota(jnp.int32, (layers, rows, width), 2)
@@ -192,7 +190,7 @@
         return out
 
     def rim_of(field, ring):
-        for side, index in ((0, 3 - ring), (1, ring - 1)):
+        for side, index in ((0, 4 - ring), (1, ring - 1)):
             for half in range(2):
                 r.rim[field, half, side, index] = r.halo[field, side, index, :, halves[half]]
         out = []
@@ -201,7 +199,7 @@
                 jnp.concatenate(
                     [
                         r.rim[field, half, side, index, pl.ds(px, rows, stride=2), :][None]
-                        for side, index in ((0, 3 - ring), (1, ring - 1))
+                        for side, index in ((0, 4 - ring), (1, ring - 1))
                     ],
                     0,
                 )
@@ -302,14 +300,6 @@
                 only,
             )
         )
-        rim_arrived += beside_copies(
-            (r.scale_buf.at[pl.ds(layers - 2, 2)], r.scale_buf.at[pl.ds(0, 2)]),
-            lambda side: r.scale_rim_in.at[d - 1, side],
-            r.scale_rim_send.at[d - 1],
-            r.scale_rim_recv.at[d - 1],
-            d,
-            only,
-        )
     control = core_of(2)
     initial = core_of(3)
     coarse_first = 0.25 * total(initial)
@@ -330,7 +320,7 @@
     swept1 = first_sweep(start1, force1, rate1, guess1, inverse1)
     swept1 = [[inside(v) for v in node] for node in swept1]
 
-    def offsets_of(swept, coarse, coarse_rim):
+    def offsets_of(swept, coarse, depth, coarse_control, rate, coarse_rate, scale):
         restricted = []
         for j in range(3):
             a, b, c, d = swept[j]
@@ -338,7 +328,7 @@
             local = [jnp.tanh(swept[j][p]) - rate[p] * swept[j][p] for p in range(4)]
             restricted.append(
                 0.25 * (diffusion * edges + total(local))
-                + diffusion * (inner(coarse[j]) - 4.0 * coarse[j] + outer(coarse_rim[j]))
+                + diffusion * (depth[j] - 4.0 * coarse[j])
                 + coarse_control
             )
         return [
@@ -367,39 +357,59 @@
 
     coarse = [0.25 * total(swept[m]) for m in range(3)]
     coarse1 = [0.25 * total(swept1[m]) for m in range(3)]
-    offset = offsets_of(swept, coarse, coarse1)
+    depth = [inner(coarse[j]) + outer(coarse1[j]) for j in range(3)]
+    offset = offsets_of(swept, coarse, depth, coarse_control, rate, coarse_rate, scale)
     core_arrived += send_offset(0, offset[2])
-    for d in range(1, slices):
-        rim_arrived += beside_copies(
-            (r.offset_buf.at[0, pl.ds(layers - 2, 2)], r.offset_buf.at[0, pl.ds(0, 2)]),
-            lambda side: r.offset_rim_in.at[d - 1, side],
-            r.offset_rim_send.at[d - 1],
-            r.offset_rim_recv.at[d - 1],
-            d,
-        )
-    for m in range(3):
-        r.own_buf[:, m] = offset[m]
-    own_arrived = beside_copies(
-        (r.own_buf.at[pl.ds(layers - 2, 2)], r.own_buf.at[pl.ds(0, 2)]),
-        lambda side: r.own_rim.at[side],
-        r.own_send,
-        r.own_recv,
-    )
     for p in range(4):
         r.end_buf[pl.ds(1, layers), p] = swept[2][p]
         r.end_buf[0, p] = swept1[2][p][0]
         r.end_buf[layers + 1, p] = swept1[2][p][1]
-    end_arrived = later_copy(1, r.end_buf, r.end_in, r.end_send, r.end_recv)
 
     for arrived in far:
         arrived()
-    guess3 = rim_of(0, 3)
+    guess3, guess4 = rim_of(0, 3), rim_of(0, 4)
     rate2, control2, initial2 = rim_of(1, 2), rim_of(2, 2), rim_of(3, 2)
+    rate3, control3, initial3 = rim_of(1, 3), rim_of(2, 3), rim_of(3, 3)
     start2 = [jnp.where(leading, initial2[p], guess2[p]) for p in range(4)]
     force2 = force_of(guess2, [guess3[p] + guess1[p] for p in range(4)], control2, rate2)
     swept2 = first_sweep(start2, force2, rate2, guess2, inverse_of(rate2))
     coarse2 = [0.25 * total(swept2[m]) for m in range(3)]
-    scale1, scale2 = scale_of(0.25 * total(rate1)), scale_of(0.25 * total(rate2))
+    start3 = [jnp.where(leading, initial3[p], guess3[p]) for p in range(4)]
+    force3 = force_of(guess3, [guess4[p] + guess2[p] for p in range(4)], control3, rate3)
+    swept3 = first_sweep(start3, force3, rate3, guess3, inverse_of(rate3))
+    coarse2 = [inside(v) for v in coarse2]
+    coarse3 = [inside(0.25 * total(swept3[m])) for m in range(3)]
+    coarse_rate1, coarse_rate2 = 0.25 * total(rate1), 0.25 * total(rate2)
+    scale1, scale2 = scale_of(coarse_rate1), scale_of(coarse_rate2)
+    offset1 = offsets_of(
+        swept1,
+        coarse1,
+        [coarse2[j] + ends_of(coarse[j]) for j in range(3)],
+        0.25 * total(control1),
+        rate1,
+        coarse_rate1,
+        scale1,
+    )
+    offset2 = offsets_of(
+        swept2,
+        coarse2,
+        [coarse3[j] + coarse1[j] for j in range(3)],
+        0.25 * total(control2),
+        rate2,
+        coarse_rate2,
+        scale2,
+    )
+    first1, first2 = 0.25 * total(initial1), 0.25 * total(initial2)
+    for k, first, scales, last in ((0, first1, scale1[2], offset1[2]), (1, first2, scale2[2], offset2[2])):
+        r.rim_buf[0, k] = scales
+        r.rim_buf[1, k] = jnp.where(leading, scales * first + last, last)
+    for d in reversed(range(1, slices)):
+        rim_arrived.append(
+            later_copy(
+                d, r.rim_buf, r.rim_in.at[d - 1], r.rim_send.at[d - 1], r.rim_recv.at[d - 1]
+            )
+        )
+    end_arrived = later_copy(1, r.end_buf, r.end_in, r.end_send, r.end_recv)
 
     for arrived in core_arrived:
         arrived()
@@ -413,31 +423,23 @@
         force_of(nodes[j], [inner(nodes[j][p]) for p in range(4)], control, rate)
         for j in range(3)
     ]
-    for arrived in rim_arrived + own_arrived:
+    for arrived in rim_arrived:
         arrived()
 
-    def ring(ref, k):
-        return jnp.concatenate([ref[0, 2 - k][None], ref[1, k - 1][None]], 0)
-
     start_rim = [
-        chain(
-            0.25 * total(initial_ring),
-            lambda d: ring(r.scale_rim_in.at[d - 1], k),
-            lambda d: ring(r.offset_rim_in.at[d - 1], k),
-        )
-        for k, initial_ring in ((1, initial1), (2, initial2))
+        chain(first, lambda d: r.rim_in[d - 1, 0, k], lambda d: r.rim_in[d - 1, 1, k])
+        for k, first in ((0, first1), (1, first2))
     ]
 
-    def rim_nodes(k, scales, coarses, sweeps):
-        own = ring(r.own_rim, k)
+    def rim_nodes(k, scales, offsets, coarses, sweeps):
         out = []
         for m in range(3):
-            corrected = scales[m] * start_rim[k - 1] + own[:, m] - coarses[m]
+            corrected = scales[m] * start_rim[k - 1] + offsets[m] - coarses[m]
             out.append([inside(sweeps[m][p] + corrected) for p in range(4)])
         return out
 
-    nodes1 = rim_nodes(1, scale1, coarse1, swept1)
-    nodes2 = rim_nodes(2, scale2, coarse2, swept2)
+    nodes1 = rim_nodes(1, scale1, offset1, coarse1, swept1)
+    nodes2 = rim_nodes(2, scale2, offset2, coarse2, swept2)
     forces = [
         [forces[j][p] + diffusion * outer(nodes1[j][p]) for p in range(4)] for j in range(3)
     ]
@@ -466,7 +468,8 @@
 
     coarse = [0.25 * total(swept[m]) for m in range(3)]
     coarse1 = [inside(0.25 * total(swept1[m])) for m in range(3)]
-    offset = offsets_of(swept, coarse, coarse1)
+    depth = [inner(coarse[j]) + outer(coarse1[j]) for j in range(3)]
+    offset = offsets_of(swept, coarse, depth, coarse_control, rate, coarse_rate, scale)
     for arrived in send_offset(1, offset[2]):
         arrived()
     coarse_start = chain(
@@ -507,16 +510,14 @@
     coarse = (layers, rows, width)
     scratch = dict(
         raw=vmem((4, 2, layers, depth_rows, width)),
-        halo=vmem((4, 2, 3, depth_rows, columns)),
-        rim=vmem((4, 2, 2, 3, depth_rows, width)),
+        halo=vmem((4, 2, 4, depth_rows, columns)),
+        rim=vmem((4, 2, 2, 4, depth_rows, width)),
         scale_buf=vmem(coarse),
         scale_in=vmem((later,) + coarse),
-        scale_rim_in=vmem((later, 2, 2, rows, width)),
         offset_buf=vmem((ITERS,) + coarse),
         offset_in=vmem((ITERS, later) + coarse),
-        offset_rim_in=vmem((later, 2, 2, rows, width)),
-        own_buf=vmem((layers, 3, rows, width)),
-        own_rim=vmem((2, 2, 3, rows, width)),
+        rim_buf=vmem((2, 2, 2, rows, width)),
+        rim_in=vmem((later, 2, 2, 2, rows, width)),
         end_buf=vmem((layers + 2, 4, rows, width)),
         end_in=vmem((layers + 2, 4, rows, width)),
         out_buf=vmem((3, 2, layers, depth_rows, width)),
@@ -526,14 +527,10 @@
         halo_recv=dma((8, 2)),
         scale_send=dma((later,)),
         scale_recv=dma((later,)),
-        scale_rim_send=dma((later, 2)),
-        scale_rim_recv=dma((later, 2)),
         offset_send=dma((ITERS, later)),
         offset_recv=dma((ITERS, later)),
-        offset_rim_send=dma((later, 2)),
-        offset_rim_recv=dma((later, 2)),
-        own_send=dma((2,)),
-        own_recv=dma((2,)),
+        rim_send=dma((later,)),
+        rim_recv=dma((later,)),
         end_send=dma,
         end_recv=dma,
     )

time: 17.7 us -> 16.9 us (0.955); the launches traced: 17.3 us -> 16.7 us
  Pallas kernels: 15.7 us -> 15.1 us
    pallas_call x1, Pallas kernels: 15.7 us -> 15.1 us  [per_device(): pl.pallas_call(body, out_shape=jax.ShapeDtypeStruct((1, 3, layers, depth_...]
where the time goes in v4:
time: 16.9 us; the launch traced here: 16.7 us
  Pallas kernels  15.1 us (89%)
  local copies, waits for them, and re-layouts  1.62 us (10%)
    pallas_call x1, Pallas kernels, per_device(): pl.pallas_call(body, out_shape=jax.ShapeDtypeStruct((1, 3, layers, depth_...  15.1 us
    unnamed x1, local copies, waits for them, and re-layouts  1.62 us

profile of v4, /device:TPU:3, one launch (start us, length us, event | category | flops | bytes accessed | tf_op | source)
XLA Modules:
  0.0 16.7 jit_solution(168271698734362688)
XLA Ops:
  0.0 15.1 %shard_map.46 = f32[1,3,4,16,256]{4,3,2,1,0:T(8,128)} custom-call(f32[4,16,256]{2,1,0:T(8,128)} %refs_0_.1, f32[1,4,16,256]{3,2,1,0:T(8,128)} %refs_1_.1, f32[1,4,16,256]{3,2,1,0:T(8,128)} %refs_2_.1, f32[1,4,16,256]{3,2,1,0:T(8,128)} %refs_3_.1), custom_call_target="tpu_custom_call" | custom-call | tf_op jit(solution)/shard_map/pallas_call | solution.py:542
  15.1 1.6 %copy.6 = f32[1,3,4,16,256]{4,3,2,1,0:T(8,128)} copy(f32[1,3,4,16,256]{4,3,2,1,0:T(8,128)} %shard_map.46) | data formatting | bytes 393216
